TPU v7x, 128 devices: a whole 4x4x4 slice. The times are simulated.
128 devices in a mesh: bin: 16 (over x, z), xline: 8 (over y, core).
Axes of the slice: x: 4, y: 4, z: 4, core: 2. Of those that a mesh axis runs over, the one named last changes fastest.
Arguments:
- traces: float32 [32, 960, 1024], P('bin', 'xline'), may hold values from -6 to 6
- decon_filter: float32 [32, 256], P('bin'), may hold values from -0.375 to 0.375
- dip_kernel: float32 [15, 31], replicated, may hold values from -0.25 to 0.25
- cmp_kernel: float32 [3, 5], replicated, may hold values from -4 to 4
- bin_map: int32 [32, 960], P('bin', 'xline'), may hold values from 0 to 511, as said below
- slot: int32 [32, 960], P('bin', 'xline'), may hold values from 0 to 119, as said below
- fold: int32 [16, 32], P('bin', 'xline'), may hold values from 1 to 120, as said below
Outputs:
- cmp_out: float32 [16, 32, 120, 1024], P('bin', 'xline')
Inputs may be any that keep to these rules, and one draw needn't show every extreme that they name: `bin_map`: every pair (bin, slot) is taken by at most one trace, the slots of a bin are 0 to its fold - 1, each taken once. The traces held by one device go to the bins of one device at most 4 at a time, and exactly 4 for one such pair from every device and into every device; every device's bins receive exactly 240 traces. Every bin has at least one trace. Offset slot of a trace within its bin, below the bin's fold. `fold`: counts of traces per bin; on every device one bin holds exactly 120.
All inputs are finite; a program needn't handle non-finite values.
Results may differ from a plain program's by a relative error of at most 0.0001.
Values sent between devices are 32-bit elements; how exact they have to be, the bound alone decides.
A program may use at most 128 MiB of HBM per device.

v0:
```python
import jax
import jax.numpy as jnp
from jax import lax
from jax.sharding import PartitionSpec as P


def extended_2(array, sides, width):
    for axis, dim in sides:
        size, length = (lax.axis_size(axis), array.shape[dim])
        up = [(i, (i + 1) % size) for i in range(size - 1)]
        down = [(j, i) for i, j in up]
        last = lax.slice_in_dim(array, length - width, length, axis=dim)
        first = lax.slice_in_dim(array, 0, width, axis=dim)
        before = lax.ppermute(last, axis, up)
        after = lax.ppermute(first, axis, down)
        array = jnp.concatenate([before, array, after], axis=dim)
    return array


def decon_matrix(filt):
    taps = filt.shape[-1]
    lag_index = (
        jnp.arange(128, dtype=jnp.int32)[None, :] + 256 - jnp.arange(384, dtype=jnp.int32)[:, None]
    )
    valid = (lag_index >= 0) & (lag_index < taps)
    clipped = jnp.clip(lag_index, 0, taps - 1)
    return jnp.where(valid, jnp.take(filt, clipped, axis=-1), jnp.float32(0.0))


def sample_windows(data, front, back):
    samples = data.shape[-1]
    blocks_count = samples // 128
    padding = [(0, 0)] * (data.ndim - 1) + [(front, back)]
    padded = jnp.pad(data, padding)
    blocks = padded.reshape(data.shape[:-1] + (blocks_count + 2, 128))
    return jnp.concatenate(
        [
            blocks[..., 0:blocks_count, :],
            blocks[..., 1 : blocks_count + 1, :],
            blocks[..., 2 : blocks_count + 2, :],
        ],
        axis=-1,
    )


def deconvolve(data, matrices):
    windows = sample_windows(data, 256, 0)
    result = jnp.einsum("snbw,swi->snbi", windows, matrices, precision=lax.Precision.HIGHEST)
    return result.reshape(data.shape)


def rank_within(target, valid, dev_count):
    onehot = (
        (target[:, None] == jnp.arange(dev_count, dtype=jnp.int32)[None, :]) & valid[:, None]
    ).astype(jnp.int32)
    return jnp.sum(jnp.cumsum(onehot, axis=0) * onehot, axis=1) - 1


def local(traces, decon_filter, dip_kernel, cmp_kernel, bin_map, slot, fold):
    shot_count, tr_dev, samples = traces.shape
    half = (dip_kernel.shape[0] - 1) // 2
    lag_count = dip_kernel.shape[1]
    lag_half = (lag_count - 1) // 2
    matrices = decon_matrix(decon_filter)
    extended = extended_2(deconvolve(traces, matrices), (("xline", 1),), half)
    sample_padded = jnp.pad(extended, ((0, 0), (0, 0), (lag_half, lag_half)))

    def add_term(trace_tap, running):
        sliced = lax.dynamic_slice_in_dim(sample_padded, trace_tap, tr_dev, 1)
        weights = lax.dynamic_index_in_dim(dip_kernel, trace_tap, 0, keepdims=False)
        for lag in range(lag_count):
            running = running + weights[lag] * sliced[:, :, lag : lag + samples]
        return running

    start = jnp.zeros((shot_count, tr_dev, samples), jnp.float32)
    filtered = lax.fori_loop(0, dip_kernel.shape[0], add_term, start).reshape(
        shot_count * tr_dev, samples
    )
    bin_devices = lax.axis_size("bin")
    cross_devices = lax.axis_size("xline")
    dev_count = bin_devices * cross_devices
    il_local, xl_local = fold.shape
    per_device = shot_count * tr_dev
    bins_local = il_local * xl_local
    send_cap = 2 * ((per_device + dev_count - 1) // dev_count)
    fold_cap = 2 * ((per_device + bins_local - 1) // bins_local)
    cross_total = xl_local * cross_devices
    global_bin = bin_map.reshape(per_device)
    slot_flat = slot.reshape(per_device)
    inline = global_bin // cross_total
    cross_bin = global_bin % cross_total
    bin_dev = inline // il_local
    cross_dev = cross_bin // xl_local
    il_in = inline % il_local
    xl_in = cross_bin % xl_local
    target = bin_dev * cross_devices + cross_dev
    always = jnp.ones((per_device,), jnp.bool_)
    dest_rank = rank_within(target, always, dev_count)
    cross_half = (cmp_kernel.shape[0] - 1) // 2
    offset_half = (cmp_kernel.shape[1] - 1) // 2
    buffer_rows = bins_local * fold_cap
    slot_code = (il_in * xl_local + xl_in) * fold_cap + slot_flat
    send_row = target * send_cap + dest_rank
    outgoing = jnp.zeros((dev_count * send_cap, samples), jnp.float32).at[send_row].set(filtered)
    out_codes = (
        jnp.full((dev_count * send_cap,), buffer_rows, jnp.int32).at[send_row].set(slot_code)
    )
    received, recv_codes = (
        lax.all_to_all(
            outgoing.reshape(dev_count, send_cap, samples),
            ("bin", "xline"),
            split_axis=0,
            concat_axis=0,
            tiled=True,
        ),
        lax.all_to_all(
            out_codes.reshape(dev_count, send_cap),
            ("bin", "xline"),
            split_axis=0,
            concat_axis=0,
            tiled=True,
        ),
    )
    gathers = (
        jnp.zeros((buffer_rows, samples), jnp.float32)
        .at[recv_codes.reshape(-1)]
        .set(received.reshape(-1, samples), mode="drop")
    )
    fold_scale = lax.rsqrt(jnp.maximum(fold, 1).astype(jnp.float32))
    normed = gathers.reshape(il_local, xl_local, fold_cap, samples) * fold_scale[:, :, None, None]
    with_rims = extended_2(normed, (("xline", 1),), cross_half)
    padded = jnp.pad(with_rims, ((0, 0), (0, 0), (offset_half, offset_half), (0, 0)))
    result = jnp.zeros((il_local, xl_local, fold_cap, samples), jnp.float32)
    for cross_tap in range(cmp_kernel.shape[0]):
        for offset_tap in range(cmp_kernel.shape[1]):
            result = (
                result
                + cmp_kernel[cross_tap, offset_tap]
                * padded[:, cross_tap : cross_tap + xl_local, offset_tap : offset_tap + fold_cap, :]
            )
    return result


def solution(mesh):
    return jax.shard_map(
        local,
        mesh=mesh,
        in_specs=(
            P("bin", "xline", None),
            P("bin", None),
            P(),
            P(),
            P("bin", "xline"),
            P("bin", "xline"),
            P("bin", "xline"),
        ),
        out_specs=P("bin", "xline", None, None),
        check_vma=False,
    )
```

profile of v0, /device:TPU:1, one launch (start us, length us, event | category | flops | bytes accessed | tf_op | source)
XLA Modules:
  0.0 797.2 jit_solution(1425300420080545196)
XLA Ops:
  5.1 163.1 %gather_fusion = f32[49152,2]{1,0:T(8,128)} fusion(f32[2,256]{0,1:T(8,128)S(1)} %copy.25, s32[49152]{0:T(1024)S(1)} %fusion.63), kind=kCustom, calls=%fused_computation | custom fusion | bytes 983040 | tf_op jit(solution)/shard_map/jit(_take)/gather | solution.py:27
  168.2 13.8 %copy.26 = f32[384,128,2]{1,0,2:T(8,128)S(1)} copy(f32[384,128,2]{2,1,0:T(8,128)} %bitcast.140) | data formatting | bytes 786432 | tf_op jit(solution)/shard_map/jit(_take)/gather | solution.py:27
  182.0 3.6 fusion.32
  187.1 4.6 collective-permute-start
  191.7 1.9 collective-permute-start.1
  196.6 10.6 %all-to-all-start = ((s32[128,1,4]{2,1,0:T(1,128)}), s32[128,1,4]{2,1,0:T(1,128)S(1)}, u32[]{:S(2)}, u32[]{:S(2)}) async-start(s32[128,1,4]{2,1,0:T(1,128)} %bitcast.7), calls=%async_computation | async-start | bytes 131072 | tf_op jit(solution)/shard_map/all_to_all | solution.py:116
  207.6 512.5 %while.14 = (s32[]{:T(128)}, f32[2,120,1024]{2,1,0:T(8,128)S(1)}, f32[15,31]{1,0:T(8,128)}, f32[2,134,1054]{2,1,0:T(8,128)S(1)}, s32[]{:T(128)}, /*index=5*/s32[...) while((s32[]{:T(128)}, f32[2,120,1024]{2,1,0:T(8,128)S(1)}, ...), condition=%wide.region_5.6_spmd.clone, body=%wide.region_4.5_spmd.clone.sunk | while | flops 15482913 | bytes 32441744 | solution.py:76
  209.7 31.9 %fusion.96 = f32[2,120,1024]{2,1,0:T(8,128)S(1)} fusion(f32[2,134,1054]{2,1,0:T(8,128)S(1)} %get-tuple-element.327, s32[]{:T(128)} %get-tuple-element.288, s32[]{:T(128)S(6)} %add.788, s32[]{:T(128)S(6)} %add.789, s32[]{:T(128)S(6)} %add.790, s32[]{:T(128)S(6)} %add.791, s32[]{:T(128)S(6)} %add.792, s32[]{:T(128)S(6)} %add.793, s32[]{:T(128)S(6)} %add.794, ...), kind=kLoop, calls=%fused_computation.5.clone.1 | loop fusion | flops 15482880 | bytes 32440568 | tf_op jit(solution)/shard_map/while/body/eval_jaxpr/add | solution.py:72
  243.7 31.9 %fusion.96 = f32[2,120,1024]{2,1,0:T(8,128)S(1)} fusion(f32[2,134,1054]{2,1,0:T(8,128)S(1)} %get-tuple-element.327, s32[]{:T(128)} %get-tuple-element.288, s32[]{:T(128)S(6)} %add.788, s32[]{:T(128)S(6)} %add.789, s32[]{:T(128)S(6)} %add.790, s32[]{:T(128)S(6)} %add.791, s32[]{:T(128)S(6)} %add.792, s32[]{:T(128)S(6)} %add.793, s32[]{:T(128)S(6)} %add.794, ...), kind=kLoop, calls=%fused_computation.5.clone.1 | loop fusion | flops 15482880 | bytes 32440568 | tf_op jit(solution)/shard_map/while/body/eval_jaxpr/add | solution.py:72
  277.7 31.9 %fusion.96 = f32[2,120,1024]{2,1,0:T(8,128)S(1)} fusion(f32[2,134,1054]{2,1,0:T(8,128)S(1)} %get-tuple-element.327, s32[]{:T(128)} %get-tuple-element.288, s32[]{:T(128)S(6)} %add.788, s32[]{:T(128)S(6)} %add.789, s32[]{:T(128)S(6)} %add.790, s32[]{:T(128)S(6)} %add.791, s32[]{:T(128)S(6)} %add.792, s32[]{:T(128)S(6)} %add.793, s32[]{:T(128)S(6)} %add.794, ...), kind=kLoop, calls=%fused_computation.5.clone.1 | loop fusion | flops 15482880 | bytes 32440568 | tf_op jit(solution)/shard_map/while/body/eval_jaxpr/add | solution.py:72
  311.8 31.9 %fusion.96 = f32[2,120,1024]{2,1,0:T(8,128)S(1)} fusion(f32[2,134,1054]{2,1,0:T(8,128)S(1)} %get-tuple-element.327, s32[]{:T(128)} %get-tuple-element.288, s32[]{:T(128)S(6)} %add.788, s32[]{:T(128)S(6)} %add.789, s32[]{:T(128)S(6)} %add.790, s32[]{:T(128)S(6)} %add.791, s32[]{:T(128)S(6)} %add.792, s32[]{:T(128)S(6)} %add.793, s32[]{:T(128)S(6)} %add.794, ...), kind=kLoop, calls=%fused_computation.5.clone.1 | loop fusion | flops 15482880 | bytes 32440568 | tf_op jit(solution)/shard_map/while/body/eval_jaxpr/add | solution.py:72
  345.8 31.9 %fusion.96 = f32[2,120,1024]{2,1,0:T(8,128)S(1)} fusion(f32[2,134,1054]{2,1,0:T(8,128)S(1)} %get-tuple-element.327, s32[]{:T(128)} %get-tuple-element.288, s32[]{:T(128)S(6)} %add.788, s32[]{:T(128)S(6)} %add.789, s32[]{:T(128)S(6)} %add.790, s32[]{:T(128)S(6)} %add.791, s32[]{:T(128)S(6)} %add.792, s32[]{:T(128)S(6)} %add.793, s32[]{:T(128)S(6)} %add.794, ...), kind=kLoop, calls=%fused_computation.5.clone.1 | loop fusion | flops 15482880 | bytes 32440568 | tf_op jit(solution)/shard_map/while/body/eval_jaxpr/add | solution.py:72
  379.8 31.9 %fusion.96 = f32[2,120,1024]{2,1,0:T(8,128)S(1)} fusion(f32[2,134,1054]{2,1,0:T(8,128)S(1)} %get-tuple-element.327, s32[]{:T(128)} %get-tuple-element.288, s32[]{:T(128)S(6)} %add.788, s32[]{:T(128)S(6)} %add.789, s32[]{:T(128)S(6)} %add.790, s32[]{:T(128)S(6)} %add.791, s32[]{:T(128)S(6)} %add.792, s32[]{:T(128)S(6)} %add.793, s32[]{:T(128)S(6)} %add.794, ...), kind=kLoop, calls=%fused_computation.5.clone.1 | loop fusion | flops 15482880 | bytes 32440568 | tf_op jit(solution)/shard_map/while/body/eval_jaxpr/add | solution.py:72
  413.8 31.9 %fusion.96 = f32[2,120,1024]{2,1,0:T(8,128)S(1)} fusion(f32[2,134,1054]{2,1,0:T(8,128)S(1)} %get-tuple-element.327, s32[]{:T(128)} %get-tuple-element.288, s32[]{:T(128)S(6)} %add.788, s32[]{:T(128)S(6)} %add.789, s32[]{:T(128)S(6)} %add.790, s32[]{:T(128)S(6)} %add.791, s32[]{:T(128)S(6)} %add.792, s32[]{:T(128)S(6)} %add.793, s32[]{:T(128)S(6)} %add.794, ...), kind=kLoop, calls=%fused_computation.5.clone.1 | loop fusion | flops 15482880 | bytes 32440568 | tf_op jit(solution)/shard_map/while/body/eval_jaxpr/add | solution.py:72
  447.8 31.9 %fusion.96 = f32[2,120,1024]{2,1,0:T(8,128)S(1)} fusion(f32[2,134,1054]{2,1,0:T(8,128)S(1)} %get-tuple-element.327, s32[]{:T(128)} %get-tuple-element.288, s32[]{:T(128)S(6)} %add.788, s32[]{:T(128)S(6)} %add.789, s32[]{:T(128)S(6)} %add.790, s32[]{:T(128)S(6)} %add.791, s32[]{:T(128)S(6)} %add.792, s32[]{:T(128)S(6)} %add.793, s32[]{:T(128)S(6)} %add.794, ...), kind=kLoop, calls=%fused_computation.5.clone.1 | loop fusion | flops 15482880 | bytes 32440568 | tf_op jit(solution)/shard_map/while/body/eval_jaxpr/add | solution.py:72
  481.8 32.2 %fusion.96 = f32[2,120,1024]{2,1,0:T(8,128)S(1)} fusion(f32[2,134,1054]{2,1,0:T(8,128)S(1)} %get-tuple-element.327, s32[]{:T(128)} %get-tuple-element.288, s32[]{:T(128)S(6)} %add.788, s32[]{:T(128)S(6)} %add.789, s32[]{:T(128)S(6)} %add.790, s32[]{:T(128)S(6)} %add.791, s32[]{:T(128)S(6)} %add.792, s32[]{:T(128)S(6)} %add.793, s32[]{:T(128)S(6)} %add.794, ...), kind=kLoop, calls=%fused_computation.5.clone.1 | loop fusion | flops 15482880 | bytes 32440568 | tf_op jit(solution)/shard_map/while/body/eval_jaxpr/add | solution.py:72
  516.1 32.2 %fusion.96 = f32[2,120,1024]{2,1,0:T(8,128)S(1)} fusion(f32[2,134,1054]{2,1,0:T(8,128)S(1)} %get-tuple-element.327, s32[]{:T(128)} %get-tuple-element.288, s32[]{:T(128)S(6)} %add.788, s32[]{:T(128)S(6)} %add.789, s32[]{:T(128)S(6)} %add.790, s32[]{:T(128)S(6)} %add.791, s32[]{:T(128)S(6)} %add.792, s32[]{:T(128)S(6)} %add.793, s32[]{:T(128)S(6)} %add.794, ...), kind=kLoop, calls=%fused_computation.5.clone.1 | loop fusion | flops 15482880 | bytes 32440568 | tf_op jit(solution)/shard_map/while/body/eval_jaxpr/add | solution.py:72
  550.5 32.2 %fusion.96 = f32[2,120,1024]{2,1,0:T(8,128)S(1)} fusion(f32[2,134,1054]{2,1,0:T(8,128)S(1)} %get-tuple-element.327, s32[]{:T(128)} %get-tuple-element.288, s32[]{:T(128)S(6)} %add.788, s32[]{:T(128)S(6)} %add.789, s32[]{:T(128)S(6)} %add.790, s32[]{:T(128)S(6)} %add.791, s32[]{:T(128)S(6)} %add.792, s32[]{:T(128)S(6)} %add.793, s32[]{:T(128)S(6)} %add.794, ...), kind=kLoop, calls=%fused_computation.5.clone.1 | loop fusion | flops 15482880 | bytes 32440568 | tf_op jit(solution)/shard_map/while/body/eval_jaxpr/add | solution.py:72
  584.8 32.2 %fusion.96 = f32[2,120,1024]{2,1,0:T(8,128)S(1)} fusion(f32[2,134,1054]{2,1,0:T(8,128)S(1)} %get-tuple-element.327, s32[]{:T(128)} %get-tuple-element.288, s32[]{:T(128)S(6)} %add.788, s32[]{:T(128)S(6)} %add.789, s32[]{:T(128)S(6)} %add.790, s32[]{:T(128)S(6)} %add.791, s32[]{:T(128)S(6)} %add.792, s32[]{:T(128)S(6)} %add.793, s32[]{:T(128)S(6)} %add.794, ...), kind=kLoop, calls=%fused_computation.5.clone.1 | loop fusion | flops 15482880 | bytes 32440568 | tf_op jit(solution)/shard_map/while/body/eval_jaxpr/add | solution.py:72
  619.2 32.2 %fusion.96 = f32[2,120,1024]{2,1,0:T(8,128)S(1)} fusion(f32[2,134,1054]{2,1,0:T(8,128)S(1)} %get-tuple-element.327, s32[]{:T(128)} %get-tuple-element.288, s32[]{:T(128)S(6)} %add.788, s32[]{:T(128)S(6)} %add.789, s32[]{:T(128)S(6)} %add.790, s32[]{:T(128)S(6)} %add.791, s32[]{:T(128)S(6)} %add.792, s32[]{:T(128)S(6)} %add.793, s32[]{:T(128)S(6)} %add.794, ...), kind=kLoop, calls=%fused_computation.5.clone.1 | loop fusion | flops 15482880 | bytes 32440568 | tf_op jit(solution)/shard_map/while/body/eval_jaxpr/add | solution.py:72
  653.5 32.2 %fusion.96 = f32[2,120,1024]{2,1,0:T(8,128)S(1)} fusion(f32[2,134,1054]{2,1,0:T(8,128)S(1)} %get-tuple-element.327, s32[]{:T(128)} %get-tuple-element.288, s32[]{:T(128)S(6)} %add.788, s32[]{:T(128)S(6)} %add.789, s32[]{:T(128)S(6)} %add.790, s32[]{:T(128)S(6)} %add.791, s32[]{:T(128)S(6)} %add.792, s32[]{:T(128)S(6)} %add.793, s32[]{:T(128)S(6)} %add.794, ...), kind=kLoop, calls=%fused_computation.5.clone.1 | loop fusion | flops 15482880 | bytes 32440568 | tf_op jit(solution)/shard_map/while/body/eval_jaxpr/add | solution.py:72
  687.9 32.2 %fusion.96 = f32[2,120,1024]{2,1,0:T(8,128)S(1)} fusion(f32[2,134,1054]{2,1,0:T(8,128)S(1)} %get-tuple-element.327, s32[]{:T(128)} %get-tuple-element.288, s32[]{:T(128)S(6)} %add.788, s32[]{:T(128)S(6)} %add.789, s32[]{:T(128)S(6)} %add.790, s32[]{:T(128)S(6)} %add.791, s32[]{:T(128)S(6)} %add.792, s32[]{:T(128)S(6)} %add.793, s32[]{:T(128)S(6)} %add.794, ...), kind=kLoop, calls=%fused_computation.5.clone.1 | loop fusion | flops 15482880 | bytes 32440568 | tf_op jit(solution)/shard_map/while/body/eval_jaxpr/add | solution.py:72
  720.1 1.9 scatter_custom_fusion.1
  723.7 9.8 %all-to-all-start.1 = ((f32[128,4,1024]{2,1,0:T(4,128)}), f32[128,4,1024]{2,1,0:T(4,128)S(1)}, u32[]{:S(2)}, u32[]{:S(2)}) async-start(f32[128,4,1024]{2,1,0:T(4,128)} %reshape.412), calls=%async_computation.1 | async-start | bytes 4194304 | tf_op jit(solution)/shard_map/all_to_all | solution.py:109
  734.9 28.9 %all-to-all-done.1 = f32[128,4,1024]{2,1,0:T(4,128)S(1)} async-done(((f32[128,4,1024]{2,1,0:T(4,128)}), f32[128,4,1024]{2,1,0:T(4,128)S(1)}, u32[]{:S(2)}, u32[]{:S(2)}) %all-to-all-start.1) | async-done | bytes 2097184 | tf_op jit(solution)/shard_map/all_to_all | solution.py:109
  763.9 1.8 reshape.444
  765.6 4.0 scatter_custom_fusion.2
  770.0 3.0 collective-permute-start.2
  773.0 1.9 collective-permute-start.3
  775.7 3.1 collective-permute-done.2
  778.8 4.4 collective-permute-done.3
  783.8 13.3 %fusion.38 = f32[1,4,120,1024]{3,2,1,0:T(8,128)} fusion(f32[1,6,124,1024]{3,2,1,0:T(8,128)S(1)} %select_maximum_fusion, f32[1,1,120,1024]{3,2,1,0:T(8,128)S(1)} %collective-permute-done.3, f32[1,4,120,1024]{3,2,1,0:T(8,128)S(1)} %broadcast_multiply_fusion, f32[1,1,120,1024]{3,2,1,0:T(8,128)S(1)} %collective-permute-done.2, f32[]{:T(128)} %bitcast.31, ...), kind=kLoop, calls=%fused_computation.79 | loop fusion | flops 15237120 | bytes 28508220 | tf_op jit(solution)/shard_map/add | solution.py:137
  (105 shorter events, 46.5 us)
Async XLA Ops:
  4.1 0.8 copy-start.4
  168.2 13.8 %copy-start = (f32[2,120,8,128]{3,2,1,0:T(8,128)S(1)}, f32[2,120,8,128]{3,2,1,0:T(8,128)}, u32[]{:S(2)}) copy-start(f32[2,120,8,128]{3,2,1,0:T(8,128)} %copy.28) | copy-start | bytes 2949124
  168.2 13.8 %copy-start.1 = (pred[384,128]{1,0:T(8,128)(4,1)S(1)}, pred[384,128]{1,0:T(8,128)(4,1)}, u32[]{:S(2)}) copy-start(pred[384,128]{1,0:T(8,128)(4,1)} %get-tuple-element.164) | copy-start | bytes 147460
  185.7 7.9 copy-start.3
  185.7 8.1 %copy-start.5 = (s32[2,120]{1,0:T(2,128)S(1)}, s32[2,120]{1,0:T(2,128)}, u32[]{:S(2)}) copy-start(s32[2,120]{1,0:T(2,128)} %param.14) | copy-start | bytes 2884
  187.1 20.1 %collective-permute-start = (f32[2,7,1024]{2,1,0:T(8,128)S(1)}, f32[2,7,1024]{2,1,0:T(8,128)S(1)}, u32[]{:S(2)}, u32[]{:S(2)}) collective-permute-start(f32[2,7,1024]{2,1,0:T(8,128)S(1)} %get-tuple-element.146), channel_id=1, source_target_pairs={{0,1},{1,2},{2,3},{3,4},{4,5},{5,6},{6,7},{8,9},{9,10},{10,11},{11... | collective-permute-start | bytes 172040 | tf_op jit(solution)/shard_map/ppermute | solution.py:14
  191.7 15.5 %collective-permute-start.1 = (f32[2,7,1024]{2,1,0:T(8,128)S(1)}, f32[2,7,1024]{2,1,0:T(8,128)S(1)}, u32[]{:S(2)}, u32[]{:S(2)}) collective-permute-start(f32[2,7,1024]{2,1,0:T(8,128)S(1)} %get-tuple-element.147), channel_id=1, source_target_pairs={{1,0},{2,1},{3,2},{4,3},{5,4},{6,5},{7,6},{9,8},{10,9},{11,10},{12... | collective-permute-start | bytes 172040 | tf_op jit(solution)/shard_map/ppermute | solution.py:15
  196.6 527.1 %all-to-all-start = ((s32[128,1,4]{2,1,0:T(1,128)}), s32[128,1,4]{2,1,0:T(1,128)S(1)}, u32[]{:S(2)}, u32[]{:S(2)}) async-start(s32[128,1,4]{2,1,0:T(1,128)} %bitcast.7), calls=%async_computation | async-start | bytes 131072 | tf_op jit(solution)/shard_map/all_to_all | solution.py:116
  723.7 9.8 %copy-start.6 = (s32[1,4]{1,0:T(1,128)S(1)}, s32[1,4]{1,0:T(1,128)}, u32[]{:S(2)}) copy-start(s32[1,4]{1,0:T(1,128)} %param.15) | copy-start | bytes 52
  723.7 40.2 %all-to-all-start.1 = ((f32[128,4,1024]{2,1,0:T(4,128)}), f32[128,4,1024]{2,1,0:T(4,128)S(1)}, u32[]{:S(2)}, u32[]{:S(2)}) async-start(f32[128,4,1024]{2,1,0:T(4,128)} %reshape.412), calls=%async_computation.1 | async-start | bytes 4194304 | tf_op jit(solution)/shard_map/all_to_all | solution.py:109
  769.9 5.0 copy-start.2
  770.0 8.7 %collective-permute-start.2 = (f32[1,1,120,1024]{3,2,1,0:T(8,128)S(1)}, f32[1,1,120,1024]{3,2,1,0:T(8,128)S(1)}, u32[]{:S(2)}, u32[]{:S(2)}) collective-permute-start(f32[1,1,120,1024]{3,2,1,0:T(8,128)S(1)} %get-tuple-element.141), channel_id=1, source_target_pairs={{0,1},{1,2},{2,3},{3,4},{4,5},{5,6},{6,7},{8,9},{9,10},{10,11},{11... | collective-permute-start | bytes 1474568 | tf_op jit(solution)/shard_map/ppermute | solution.py:14
  773.0 10.1 %collective-permute-start.3 = (f32[1,1,120,1024]{3,2,1,0:T(8,128)S(1)}, f32[1,1,120,1024]{3,2,1,0:T(8,128)S(1)}, u32[]{:S(2)}, u32[]{:S(2)}) collective-permute-start(f32[1,1,120,1024]{3,2,1,0:T(8,128)S(1)} %get-tuple-element.142), channel_id=1, source_target_pairs={{1,0},{2,1},{3,2},{4,3},{5,4},{6,5},{7,6},{9,8},{10,9},{11,10},{12... | collective-permute-start | bytes 1474568 | tf_op jit(solution)/shard_map/ppermute | solution.py:15
where the time goes:
time: 802 us; the launch traced here: 797 us
  other arithmetic  497 us (62%)
  local copies, waits for them, and re-layouts  227 us (28%)
  waiting for transfers between devices  36.4 us (5%)
  starting transfers between devices  31.7 us (4%)
    add x15, other arithmetic, add_term(): running = running + weights[lag] * sliced[:, :, lag:lag + samples]  480 us
    gather x2, local copies, waits for them, and re-layouts, decon_matrix(): return jnp.where(valid, jnp.take(filt, clipped, axis=-1), jnp.float32(0.0))  177 us
    all_to_all x1, waiting for transfers between devices, local(): lax.all_to_all(outgoing.reshape(dev_count, send_cap, samples), ('bin', 'x...  28.9 us
    slice x30, local copies, waits for them, and re-layouts, add_term(): running = running + weights[lag] * sliced[:, :, lag:lag + samples]  21.4 us
  transfers between devices with their start and end apart: 6, of which 3 were waited for; matrix products, arithmetic and copies ran while one was open for 65% of the time, Pallas kernels for 0%

commit v1 on v0

v1 whole, which is shorter than its diff:
```python
import functools

import jax
import jax.numpy as jnp
from jax import lax
from jax.experimental import pallas as pl
from jax.experimental.pallas import tpu as pltpu
from jax.sharding import PartitionSpec as P

MESH = pl.DeviceIdType.MESH
F32 = jnp.float32
BF16 = jnp.bfloat16
LANES = 128
GROUP = 4
STEP = 64
LEFT = 32
CHUNK = 256
PAD = 8


def iota(shape, dim):
    return lax.broadcasted_iota(jnp.int32, shape, dim)


def halves(x):
    high = x.astype(BF16)
    low = (x - high.astype(F32)).astype(BF16)
    return high, low


def dot(a, b):
    return jnp.dot(a, b, preferred_element_type=F32)


def dot3(ah, al, bh, bl):
    return dot(ah, bh) + (dot(ah, bl) + dot(al, bh))


def exact(a, b):
    return jnp.dot(a, b, preferred_element_type=F32, precision=lax.Precision.HIGHEST)


def rows_by_columns(a, b):
    return lax.dot_general(a, b, (((1,), (1,)), ((), ())), preferred_element_type=F32)


def kernel(
    dims,
    traces_ref,
    filt_ref,
    dip_ref,
    bin_ref,
    slot_ref,
    cmp_ref,
    fold_ref,
    out_ref,
    xe,
    amat_h,
    amat_l,
    dipx,
    tmat_h,
    tmat_l,
    dec,
    dec_a,
    dec_b,
    xh,
    xl,
    pick,
    code_send,
    code_recv,
    codes,
    send,
    recv,
    w_h,
    w_l,
    rim_send,
    rim_recv,
    outbuf,
    in_sem,
    halo_ssem,
    halo_rsem,
    code_ssem,
    code_rsem,
    ssem,
    rsem,
    rim_ssem,
    rim_rsem,
    out_sem,
):
    nb, nx, shots, trs, samples, cap, il, xloc, fold_cap = dims
    nd = nb * nx
    blocks = samples // LANES
    chunks = samples // CHUNK
    bi, xi = lax.axis_index("bin"), lax.axis_index("xline")
    me = bi * nx + xi
    taps = filt_ref.shape[1]
    xtaps, ltaps = dip_ref.shape
    ctaps, otaps = cmp_ref.shape
    half = (xtaps - 1) // 2
    members = xtaps + GROUP - 1
    groups = 32
    slots = nd * cap
    cols = shots * LANES

    def device(d):
        return (lax.div(d, nx), lax.rem(d, nx))

    barrier = pltpu.get_barrier_semaphore()

    def announce(k, carry):
        pl.semaphore_signal(
            barrier, inc=1, device_id=device(lax.rem(me + k, nd)), device_id_type=MESH
        )
        return carry

    lax.fori_loop(1, nd, announce, 0)

    load = pltpu.make_async_copy(
        traces_ref, xe.at[:, pl.ds(PAD, trs), pl.ds(taps, samples)], in_sem
    )
    load.start()

    xe[:, :, 0:taps] = jnp.zeros((shots, xe.shape[1], taps), F32)
    xe[:, PAD + trs + PAD :, taps:] = jnp.zeros(
        (shots, xe.shape[1] - 2 * PAD - trs, samples), F32
    )

    @pl.when(xi == 0)
    def _():
        xe[:, 0:PAD, taps:] = jnp.zeros((shots, PAD, samples), F32)

    @pl.when(xi == nx - 1)
    def _():
        xe[:, PAD + trs : PAD + trs + PAD, taps:] = jnp.zeros((shots, PAD, samples), F32)

    lane = iota((1, LANES), 1)
    bins = bin_ref[...]
    xl_bits = (xloc * nx).bit_length() - 1
    loc_bits = xloc.bit_length() - 1
    inline = lax.shift_right_logical(bins, xl_bits)
    cross = bins & (xloc * nx - 1)
    target = inline // il if il > 1 else inline
    target = target * nx + lax.shift_right_logical(cross, loc_bits)
    local_bin = cross & (xloc - 1)
    if il > 1:
        local_bin = local_bin + (inline % il) * xloc
    pad_cols = jnp.zeros((shots, LANES - trs), F32)
    table = jnp.concatenate(
        [
            jnp.concatenate([x.astype(F32), pad_cols], axis=1)
            for x in (target + 1, local_bin + 1, slot_ref[...] + 1)
        ]
        + [jnp.zeros((8 - 3 * shots, LANES), F32)],
        axis=0,
    )
    r_i, n_i = iota((LANES, LANES), 0), iota((LANES, LANES), 1)
    order = jnp.where(r_i == GROUP * (n_i & (groups - 1)) + lax.shift_right_logical(n_i, 5), 1.0, 0.0)
    table = exact(table, order.astype(F32))

    def row(kind):
        return jnp.concatenate([table[kind * shots + s : kind * shots + s + 1] for s in range(shots)], axis=1)

    t_row = row(0).astype(jnp.int32) - 1
    b_row, s_row = row(1), row(2)
    onehot = (iota((nd, cols), 0) == t_row).astype(F32)
    onehot_b = onehot.astype(BF16)
    before = (iota((cols, cols), 0) < iota((cols, cols), 1)).astype(F32).astype(BF16)
    rank = jnp.sum(onehot * dot(onehot_b, before), axis=0, keepdims=True)
    rank = (rank + 0.5).astype(jnp.int32)
    pick[...] = (iota((slots, cols), 0) == t_row * cap + rank).astype(F32).astype(BF16)
    k_i = iota((LANES, cols), 0)
    coded = jnp.where(
        k_i == rank, b_row, jnp.where(k_i == rank + cap, s_row, jnp.zeros((LANES, cols), F32))
    )
    coded = jnp.where(k_i < 2 * cap, coded, 0.0)
    outgoing_codes = rows_by_columns(onehot_b, coded.astype(BF16))
    for d in range(nd):
        code_send[d] = outgoing_codes[d : d + 1]

    for s in range(shots):
        base = jnp.concatenate([jnp.zeros((1, taps), F32), filt_ref[s : s + 1]], axis=1)
        rolled = pltpu.roll(
            jnp.broadcast_to(base, (LANES, 2 * taps)), 0, 1, stride=1, stride_axis=0
        )
        k_b, i_b = iota((LANES, LANES), 0), iota((LANES, LANES), 1)
        kinds = {
            0: jnp.where(i_b < k_b, rolled[:, 0:LANES], 0.0),
            1: rolled[:, 3 * LANES : 4 * LANES],
            2: rolled[:, 2 * LANES : 3 * LANES],
        }
        for kb in range(4):
            for ib in range(2):
                block = kinds.get(kb - ib, jnp.zeros((LANES, LANES), F32))
                high, low = halves(block)
                place = (s, pl.ds(kb * LANES, LANES), pl.ds(ib * LANES, LANES))
                amat_h[place] = high
                amat_l[place] = low

    dipx[...] = jnp.zeros(dipx.shape, F32)
    dipx[0:xtaps, 0:ltaps] = dip_ref[...]
    dipx[1 : xtaps + 1, LANES : LANES + ltaps] = dip_ref[...]
    lhalf = (ltaps - 1) // 2
    near = LEFT - lhalf
    l_i, m_i = iota((2 * LANES, LANES), 0), iota((2 * LANES, LANES), 1)
    first = (l_i < ltaps) & (m_i == LANES - near - l_i)
    second = (l_i >= LANES) & (l_i < LANES + ltaps) & (m_i == STEP - near - (l_i - LANES))
    rows16 = exact(dipx[...], jnp.where(first | second, 1.0, 0.0).astype(F32))
    k_b, i_b = iota((LANES, LANES), 0), iota((LANES, LANES), 1)
    delta = k_b - (i_b & (STEP - 1)) - near
    band = (delta >= 0) & (delta < ltaps)
    zero_block = jnp.zeros((LANES, LANES), BF16)
    for u in (0, 1):
        tmat_h[u * LANES : (u + 1) * LANES, LANES:] = zero_block
        tmat_l[u * LANES : (u + 1) * LANES, LANES:] = zero_block
    for u in (members - 2, members - 1):
        tmat_h[u * LANES : (u + 1) * LANES, 0:LANES] = zero_block
        tmat_l[u * LANES : (u + 1) * LANES, 0:LANES] = zero_block
    for v in range(xtaps + 1):
        rolled = pltpu.roll(
            jnp.broadcast_to(rows16[v : v + 1], (LANES, LANES)), 0, 1, stride=1, stride_axis=0
        )
        high, low = halves(jnp.where(band, rolled, 0.0))
        for u, at in ((v, 0), (v + 2, LANES)):
            tmat_h[u * LANES : (u + 1) * LANES, at : at + LANES] = high
            tmat_l[u * LANES : (u + 1) * LANES, at : at + LANES] = low

    load.wait()
    pl.semaphore_wait(barrier, nd - 1)

    def halo(side):
        at = PAD if side == 0 else trs
        to = PAD + trs if side == 0 else 0
        return pltpu.make_async_remote_copy(
            src_ref=xe.at[:, pl.ds(at, PAD), pl.ds(taps, samples)],
            dst_ref=xe.at[:, pl.ds(to, PAD), pl.ds(taps, samples)],
            send_sem=halo_ssem.at[side],
            recv_sem=halo_rsem.at[side],
            device_id=(bi, xi - 1 if side == 0 else xi + 1),
            device_id_type=MESH,
        )

    has_left, has_right = xi > 0, xi < nx - 1

    @pl.when(has_left)
    def _():
        halo(0).start()

    @pl.when(has_right)
    def _():
        halo(1).start()

    def send_codes(k, carry):
        d = lax.rem(me + k, nd)
        pltpu.make_async_remote_copy(
            src_ref=code_send.at[d],
            dst_ref=code_recv.at[me],
            send_sem=code_ssem,
            recv_sem=code_rsem,
            device_id=device(d),
            device_id_type=MESH,
        ).start()
        return carry

    lax.fori_loop(1, nd, send_codes, 0)

    dec[:, 0] = jnp.zeros((shots,) + dec.shape[2:], F32)
    dec[:, blocks + 1] = jnp.zeros((shots,) + dec.shape[2:], F32)

    def deconvolve(at, rows):
        for s in range(shots):
            window = xe[s, pl.ds(at, rows), :]
            high, low = halves(window)
            for n in range(samples // taps):
                part = slice(n * taps, n * taps + 2 * taps)
                got = dot3(high[:, part], low[:, part], amat_h[s], amat_l[s])
                for e in range(taps // LANES):
                    dec[s, 1 + n * (taps // LANES) + e, pl.ds(at, rows), :] = got[
                        :, e * LANES : (e + 1) * LANES
                    ]

    deconvolve(PAD, trs + 0)

    @pl.when(has_right)
    def _():
        halo(0).wait_recv()

    @pl.when(has_left)
    def _():
        halo(1).wait_recv()

    deconvolve(0, PAD)
    deconvolve(PAD + trs, 2 * PAD)

    @pl.when(has_left)
    def _():
        halo(0).wait_send()

    @pl.when(has_right)
    def _():
        halo(1).wait_send()

    def shift_block(e, carry):
        for s in range(shots):
            here = dec[s, e + 1]
            l_b = iota(here.shape, 1)
            dec_a[s, e] = jnp.where(
                l_b < LEFT, pltpu.roll(dec[s, e], LEFT, 1), pltpu.roll(here, LEFT, 1)
            )
            dec_b[s, e] = jnp.where(
                l_b < LANES - LEFT,
                pltpu.roll(here, LANES - LEFT, 1),
                pltpu.roll(dec[s, e + 2], LANES - LEFT, 1),
            )
        return carry

    lax.fori_loop(0, blocks, shift_block, 0)

    per = CHUNK // LANES
    sub = iota((8, LANES), 0)

    def dip_and_send(c, carry):
        for s in range(shots):
            for e in range(per):
                for parity, source in enumerate((dec_a, dec_b)):
                    at = ((s * per + e) * 2 + parity) * groups
                    for u in range(members):
                        piece = source[
                            s, c * per + e, pl.ds(PAD - half + u, groups, stride=GROUP), :
                        ]
                        high, low = halves(piece)
                        xh[at : at + groups, u * LANES : (u + 1) * LANES] = high
                        xl[at : at + groups, u * LANES : (u + 1) * LANES] = low
        got = dot3(xh[...], xl[...], tmat_h[...], tmat_l[...])
        columns = []
        l_g = iota((groups, LANES), 1)
        for e in range(per):
            stack = []
            for s in range(shots):
                for p in range(GROUP):
                    pp = slice((p // 2) * LANES, (p // 2) * LANES + LANES)
                    at = ((s * per + e) * 2) * groups
                    even = got[at : at + groups, pp]
                    odd = got[at + groups : at + 2 * groups, pp]
                    if p % 2 == 0:
                        stack.append(jnp.where(l_g < STEP, even, pltpu.roll(odd, STEP, 1)))
                    else:
                        stack.append(jnp.where(l_g < STEP, pltpu.roll(even, STEP, 1), odd))
            columns.append(jnp.concatenate(stack, axis=0))
        high, low = halves(jnp.concatenate(columns, axis=1))
        packed = dot(pick[...], high) + dot(pick[...], low)
        for pair in range(nd // 2):
            a = packed[8 * pair : 8 * pair + 8, 0:LANES]
            b = packed[8 * pair : 8 * pair + 8, LANES:]
            send[c, 16 * pair : 16 * pair + 8] = jnp.where(sub < 4, a, pltpu.roll(b, 4, 0))
            send[c, 16 * pair + 8 : 16 * pair + 16] = jnp.where(sub < 4, pltpu.roll(a, 4, 0), b)
        own = pl.ds(pl.multiple_of(me * 8, 8), 8)
        recv[c, own, :] = send[c, own, :]

        def start(k, carry):
            d = lax.rem(me + k, nd)
            pltpu.make_async_remote_copy(
                src_ref=send.at[c, pl.ds(pl.multiple_of(d * 8, 8), 8)],
                dst_ref=recv.at[c, own],
                send_sem=ssem.at[c],
                recv_sem=rsem.at[c],
                device_id=device(d),
                device_id_type=MESH,
            ).start()
            return carry

        lax.fori_loop(1, nd, start, 0)
        return carry

    lax.fori_loop(0, chunks, dip_and_send, 0)

    code_recv[me] = code_send[me]
    some = code_recv.at[pl.ds(0, nd - 1)]
    pltpu.make_async_copy(some, some, code_rsem).wait()
    some = code_send.at[pl.ds(0, nd - 1)]
    pltpu.make_async_copy(some, some, code_ssem).wait()
    for d in range(nd):
        codes[d : d + 1, :] = code_recv[d]
    eye = (iota((8, LANES), 0) == iota((8, LANES), 1)).astype(F32).astype(BF16)
    by_slot = rows_by_columns(eye, codes[...].astype(BF16)).astype(BF16)
    r_l = iota((nd, slots), 1)
    spread = (lax.shift_right_logical(r_l, 2) == iota((nd, slots), 0)).astype(F32).astype(BF16)
    spread = dot(by_slot, spread)
    k_s = iota((8, slots), 0)
    own_k = iota((8, slots), 1) & (cap - 1)
    in_bin = jnp.sum(jnp.where(k_s == own_k, spread, 0.0), axis=0, keepdims=True) - 1.0
    in_slot = jnp.sum(jnp.where(k_s == own_k + cap, spread, 0.0), axis=0, keepdims=True) - 1.0
    in_bin = jnp.where(in_bin < 0.0, in_bin - 0.5, in_bin + 0.5).astype(jnp.int32)
    in_slot = (in_slot + 1.5).astype(jnp.int32) - 1
    in_slot = jnp.where(in_bin < 0, -1000, in_slot)
    folds = jnp.ones(in_bin.shape, jnp.int32)
    for b in range(xloc):
        folds = jnp.where(in_bin == b, fold_ref[0, b], folds)
    scale = lax.rsqrt(jnp.maximum(folds, 1).astype(F32))
    chalf, ohalf = (ctaps - 1) // 2, (otaps - 1) // 2
    line = [-1, xloc] + list(range(xloc))
    weights = []
    for c in line:
        per_tap = []
        for o in range(otaps):
            w = jnp.zeros(in_bin.shape, F32)
            for b in range(xloc):
                a = b - c + chalf
                if 0 <= a < ctaps:
                    w = jnp.where(in_bin == b, cmp_ref[a, o], w)
            per_tap.append(w * scale)
        weights.append(per_tap)

    def fill_weights(ft, carry):
        offset = in_slot - (ft * 16 + iota((16, slots), 0))
        hits = [offset == o - ohalf for o in range(otaps)]
        for ci in range(len(line)):
            w = jnp.zeros((16, slots), F32)
            for o in range(otaps):
                w = jnp.where(hits[o], weights[ci][o], w)
            high, low = halves(w)
            at = pl.ds(pl.multiple_of(ci * LANES + ft * 16, 16), 16)
            w_h[at, :] = high
            w_l[at, :] = low
        return carry

    lax.fori_loop(0, LANES // 16, fill_weights, 0)

    def rim(c, side):
        return pltpu.make_async_remote_copy(
            src_ref=rim_send.at[c, side],
            dst_ref=rim_recv.at[c, side],
            send_sem=rim_ssem.at[c, side],
            recv_sem=rim_rsem.at[c, side],
            device_id=(bi, xi - 1 if side == 0 else xi + 1),
            device_id_type=MESH,
        )

    def gather(c, carry):
        some = recv.at[c, pl.ds(0, 8 * (nd - 1))]
        pltpu.make_async_copy(some, some, rsem.at[c]).wait()
        first, second = [], []
        for pair in range(nd // 2):
            a = recv[c, 16 * pair : 16 * pair + 8]
            b = recv[c, 16 * pair + 8 : 16 * pair + 16]
            first.append(jnp.where(sub < 4, a, pltpu.roll(b, 4, 0)))
            second.append(jnp.where(sub < 4, pltpu.roll(a, 4, 0), b))
        whole = jnp.concatenate(
            [jnp.concatenate(first, axis=0), jnp.concatenate(second, axis=0)], axis=1
        )
        high, low = halves(whole)
        edge = dot3(w_h[0 : 2 * LANES], w_l[0 : 2 * LANES], high, low)
        rim_send[c, 0] = edge[0:fold_cap]
        rim_send[c, 1] = edge[LANES : LANES + fold_cap]

        @pl.when(has_left)
        def _():
            rim(c, 0).start()

        @pl.when(has_right)
        def _():
            rim(c, 1).start()

        for b in range(xloc):
            at = (2 + b) * LANES
            outbuf[c, b] = dot3(w_h[at : at + LANES], w_l[at : at + LANES], high, low)[0:fold_cap]
        return carry

    lax.fori_loop(0, chunks, gather, 0)

    def finish(c, carry):
        @pl.when(has_right)
        def _():
            rim(c, 0).wait_recv()
            outbuf[c, xloc - 1] += rim_recv[c, 0]

        @pl.when(has_left)
        def _():
            rim(c, 1).wait_recv()
            outbuf[c, 0] += rim_recv[c, 1]

        store(c).start()
        return carry

    def store(c):
        return pltpu.make_async_copy(
            outbuf.at[c],
            out_ref.at[0, :, :, pl.ds(pl.multiple_of(c * CHUNK, CHUNK), CHUNK)],
            out_sem.at[c],
        )

    lax.fori_loop(0, chunks, finish, 0)

    def drain(c, carry):
        some = send.at[c, pl.ds(0, 8 * (nd - 1))]
        pltpu.make_async_copy(some, some, ssem.at[c]).wait()

        @pl.when(has_left)
        def _():
            rim(c, 0).wait_send()

        @pl.when(has_right)
        def _():
            rim(c, 1).wait_send()

        store(c).wait()
        return carry

    lax.fori_loop(0, chunks, drain, 0)


def local(nb, nx, traces, decon_filter, dip_kernel, cmp_kernel, bin_map, slot, fold):
    shots, trs, samples = traces.shape
    il, xloc = fold.shape
    nd = nb * nx
    cap = 2 * -(-(shots * trs) // nd)
    fold_cap = 2 * -(-(shots * trs) // (il * xloc))
    taps = decon_filter.shape[1]
    dims = (nb, nx, shots, trs, samples, cap, il, xloc, fold_cap)
    assert il == 1 and cap == 4 and taps == 2 * LANES
    members = dip_kernel.shape[0] + GROUP - 1
    blocks, chunks = samples // LANES, samples // CHUNK
    rows = trs + 3 * PAD
    slots = nd * cap
    m_rows = shots * (CHUNK // STEP) * 32
    vmem = pl.BlockSpec(memory_space=pltpu.VMEM)
    smem = pl.BlockSpec(memory_space=pltpu.SMEM)
    hbm = pl.BlockSpec(memory_space=pl.ANY)
    dma, regular = pltpu.SemaphoreType.DMA, pltpu.SemaphoreType.REGULAR
    return pl.pallas_call(
        functools.partial(kernel, dims),
        out_shape=jax.ShapeDtypeStruct((il, xloc, fold_cap, samples), F32),
        in_specs=[hbm, vmem, vmem, vmem, vmem, smem, smem],
        out_specs=hbm,
        scratch_shapes=[
            pltpu.VMEM((shots, rows, taps + samples), F32),
            pltpu.VMEM((shots, 2 * taps, taps), BF16),
            pltpu.VMEM((shots, 2 * taps, taps), BF16),
            pltpu.VMEM((dip_kernel.shape[0] + 1, 2 * LANES), F32),
            pltpu.VMEM((members * LANES, 2 * LANES), BF16),
            pltpu.VMEM((members * LANES, 2 * LANES), BF16),
            pltpu.VMEM((shots, blocks + 2, rows, LANES), F32),
            pltpu.VMEM((shots, blocks, rows, LANES), F32),
            pltpu.VMEM((shots, blocks, rows, LANES), F32),
            pltpu.VMEM((m_rows, members * LANES), BF16),
            pltpu.VMEM((m_rows, members * LANES), BF16),
            pltpu.VMEM((slots, shots * LANES), BF16),
            pltpu.VMEM((nd, 1, LANES), F32),
            pltpu.VMEM((nd, 1, LANES), F32),
            pltpu.VMEM((nd, LANES), F32),
            pltpu.VMEM((chunks, nd * 8, LANES), F32),
            pltpu.VMEM((chunks, nd * 8, LANES), F32),
            pltpu.VMEM(((xloc + 2) * LANES, slots), BF16),
            pltpu.VMEM(((xloc + 2) * LANES, slots), BF16),
            pltpu.VMEM((chunks, 2, fold_cap, CHUNK), F32),
            pltpu.VMEM((chunks, 2, fold_cap, CHUNK), F32),
            pltpu.VMEM((chunks, xloc, fold_cap, CHUNK), F32),
            dma,
            dma((2,)),
            dma((2,)),
            dma,
            dma,
            dma((chunks,)),
            dma((chunks,)),
            dma((chunks, 2)),
            dma((chunks, 2)),
            dma((chunks,)),
        ],
        compiler_params=pltpu.CompilerParams(
            collective_id=0, has_side_effects=True, vmem_limit_bytes=48 << 20
        ),
    )(traces, decon_filter, dip_kernel, bin_map, slot, cmp_kernel, fold)


def solution(mesh):
    return jax.shard_map(
        functools.partial(local, mesh.shape["bin"], mesh.shape["xline"]),
        mesh=mesh,
        in_specs=(
            P("bin", "xline", None),
            P("bin", None),
            P(),
            P(),
            P("bin", "xline"),
            P("bin", "xline"),
            P("bin", "xline"),
        ),
        out_specs=P("bin", "xline", None, None),
        check_vma=False,
    )
```

time: 802 us -> 58.6 us (0.07)
  the two profiles are of different devices: /device:TPU:1 before, /device:TPU:3 now
where the time goes in v1:
time: 58.6 us; the launch traced here: 58.4 us
  Pallas kernels  51.8 us (88%)
  local copies, waits for them, and re-layouts  6.55 us (11%)
    pallas_call x1, Pallas kernels, local(): pl.pallas_call(functools.partial(kernel, dims), out_shape=jax.ShapeDtypeS...  51.8 us
    unnamed x15, local copies, waits for them, and re-layouts  6.55 us

profile of v1, /device:TPU:3, one launch (start us, length us, event | category | flops | bytes accessed | tf_op | source)
XLA Modules:
  0.0 58.4 jit_solution(13572412072681794416)
XLA Ops:
  0.0 0.0 copy-start
  0.0 1.2 %copy-done = f32[2,120,1024]{2,1,0:T(8,128)S(1)} copy-done((f32[2,120,1024]{2,1,0:T(8,128)S(1)}, f32[2,120,1024]{2,1,0:T(8,128)}, u32[]{:S(2)}) %copy-start) | copy-done | bytes 983064
  1.2 0.0 copy-start.1
  1.2 0.7 %copy-done.1 = f32[15,31]{1,0:T(8,128)S(1)} copy-done((f32[15,31]{1,0:T(8,128)S(1)}, f32[15,31]{1,0:T(8,128)}, u32[]{:S(2)}) %copy-start.1) | copy-done | bytes 1884
  1.9 0.0 copy-start.2
  1.9 0.7 %copy-done.2 = f32[2,256]{1,0:T(2,128)S(1)} copy-done((f32[2,256]{1,0:T(2,128)S(1)}, f32[2,256]{1,0:T(2,128)}, u32[]{:S(2)}) %copy-start.2) | copy-done | bytes 2072
  2.6 0.0 copy-start.3
  2.6 0.7 %copy-done.3 = f32[3,5]{1,0:T(4,128)S(1)} copy-done((f32[3,5]{1,0:T(4,128)S(1)}, f32[3,5]{1,0:T(4,128)}, u32[]{:S(2)}) %copy-start.3) | copy-done | bytes 84
  3.3 0.0 copy-start.4
  3.3 0.7 %copy-done.4 = s32[2,120]{1,0:T(2,128)S(1)} copy-done((s32[2,120]{1,0:T(2,128)S(1)}, s32[2,120]{1,0:T(2,128)}, u32[]{:S(2)}) %copy-start.4) | copy-done | bytes 984
  3.9 0.0 copy-start.5
  3.9 0.7 %copy-done.5 = s32[2,120]{1,0:T(2,128)S(1)} copy-done((s32[2,120]{1,0:T(2,128)S(1)}, s32[2,120]{1,0:T(2,128)}, u32[]{:S(2)}) %copy-start.5) | copy-done | bytes 984
  4.6 0.0 copy-start.6
  4.6 0.7 %copy-done.6 = s32[1,4]{1,0:T(1,128)S(1)} copy-done((s32[1,4]{1,0:T(1,128)S(1)}, s32[1,4]{1,0:T(1,128)}, u32[]{:S(2)}) %copy-start.6) | copy-done | bytes 40
  5.3 51.8 %shard_map.73 = f32[1,4,120,1024]{3,2,1,0:T(8,128)S(1)} custom-call(f32[2,120,1024]{2,1,0:T(8,128)S(1)} %copy-done, f32[2,256]{1,0:T(2,128)S(1)} %copy-done.2, f32[15,31]{1,0:T(8,128)S(1)} %copy-done.1, s32[2,120]{1,0:T(2,128)S(1)} %copy-done.4, s32[2,120]{1,0:T(2,128)S(1)} %copy-done.5, f32[3,5]{1,0:T(4,128)S(1)} %copy-done.3, s32[1,4]{1,0:T(1,128)S(1)} %copy-done.6), custom_call_target="tpu_custom_call" | custom-call | tf_op jit(solution)/shard_map/pallas_call | solution.py:529
  57.1 1.3 %copy.9 = f32[1,4,120,1024]{3,2,1,0:T(8,128)} copy(f32[1,4,120,1024]{3,2,1,0:T(8,128)S(1)} %shard_map.73) | data formatting | bytes 3932160
Async XLA Ops:
  0.0 1.2 %copy-start = (f32[2,120,1024]{2,1,0:T(8,128)S(1)}, f32[2,120,1024]{2,1,0:T(8,128)}, u32[]{:S(2)}) copy-start(f32[2,120,1024]{2,1,0:T(8,128)} %traces_ref.1) | copy-start | bytes 2949124
  1.2 0.7 %copy-start.1 = (f32[15,31]{1,0:T(8,128)S(1)}, f32[15,31]{1,0:T(8,128)}, u32[]{:S(2)}) copy-start(f32[15,31]{1,0:T(8,128)} %dip_ref.1) | copy-start | bytes 5584
  1.9 0.7 %copy-start.2 = (f32[2,256]{1,0:T(2,128)S(1)}, f32[2,256]{1,0:T(2,128)}, u32[]{:S(2)}) copy-start(f32[2,256]{1,0:T(2,128)} %filt_ref.1) | copy-start | bytes 6148
  2.6 0.7 %copy-start.3 = (f32[3,5]{1,0:T(4,128)S(1)}, f32[3,5]{1,0:T(4,128)}, u32[]{:S(2)}) copy-start(f32[3,5]{1,0:T(4,128)} %cmp_ref.1) | copy-start | bytes 184
  3.3 0.7 %copy-start.4 = (s32[2,120]{1,0:T(2,128)S(1)}, s32[2,120]{1,0:T(2,128)}, u32[]{:S(2)}) copy-start(s32[2,120]{1,0:T(2,128)} %bin_ref.1) | copy-start | bytes 2884
  3.9 0.7 %copy-start.5 = (s32[2,120]{1,0:T(2,128)S(1)}, s32[2,120]{1,0:T(2,128)}, u32[]{:S(2)}) copy-start(s32[2,120]{1,0:T(2,128)} %slot_ref.1) | copy-start | bytes 2884
  4.6 0.7 %copy-start.6 = (s32[1,4]{1,0:T(1,128)S(1)}, s32[1,4]{1,0:T(1,128)}, u32[]{:S(2)}) copy-start(s32[1,4]{1,0:T(1,128)} %fold_ref.1) | copy-start | bytes 52

commit v2 on v1

--- a/solution.py
+++ b/solution.py
@@ -47,20 +47,26 @@
 def kernel(
     dims,
     traces_ref,
+    filt_hbm,
+    dip_hbm,
+    bin_hbm,
+    slot_hbm,
+    cmp_hbm,
+    fold_hbm,
+    out_ref,
     filt_ref,
     dip_ref,
     bin_ref,
     slot_ref,
     cmp_ref,
     fold_ref,
-    out_ref,
     xe,
     amat_h,
     amat_l,
     dipx,
     tmat_h,
     tmat_l,
-    dec,
+    last,
     dec_a,
     dec_b,
     xh,
@@ -76,7 +82,9 @@
     rim_send,
     rim_recv,
     outbuf,
+    stage_sem,
     in_sem,
+    small_sem,
     halo_ssem,
     halo_rsem,
     code_ssem,
@@ -103,18 +111,34 @@
     cols = shots * LANES
 
     def device(d):
-        return (lax.div(d, nx), lax.rem(d, nx))
+        return (lax.shift_right_logical(d, nx.bit_length() - 1), d & (nx - 1))
 
     barrier = pltpu.get_barrier_semaphore()
 
-    def announce(k, carry):
-        pl.semaphore_signal(
-            barrier, inc=1, device_id=device(lax.rem(me + k, nd)), device_id_type=MESH
+    nbz = 4
+    nbx = nb // nbz
+    xb, zb = lax.div(bi, nbz), lax.rem(bi, nbz)
+    x_peers = [(lax.rem(xb + k, nbx) * nbz + zb, xi) for k in range(1, nbx)]
+    z_peers = [(xb * nbz + lax.rem(zb + k, nbz), xi) for k in range(1, nbz)]
+    y_peers = [(bi, lax.rem(xi + k, nx)) for k in range(1, nx)]
+    for peer in y_peers + z_peers + x_peers:
+        pl.semaphore_signal(barrier, inc=1, device_id=peer, device_id_type=MESH)
+
+    smalls = [
+        pltpu.make_async_copy(a, b, small_sem.at[i])
+        for i, (a, b) in enumerate(
+            (
+                (bin_hbm, bin_ref),
+                (slot_hbm, slot_ref),
+                (filt_hbm, filt_ref),
+                (dip_hbm, dip_ref),
+                (cmp_hbm, cmp_ref),
+                (fold_hbm, fold_ref),
+            )
         )
-        return carry
-
-    lax.fori_loop(1, nd, announce, 0)
-
+    ]
+    for copy in smalls:
+        copy.start()
     load = pltpu.make_async_copy(
         traces_ref, xe.at[:, pl.ds(PAD, trs), pl.ds(taps, samples)], in_sem
     )
@@ -133,49 +157,8 @@
     def _():
         xe[:, PAD + trs : PAD + trs + PAD, taps:] = jnp.zeros((shots, PAD, samples), F32)
 
-    lane = iota((1, LANES), 1)
-    bins = bin_ref[...]
-    xl_bits = (xloc * nx).bit_length() - 1
-    loc_bits = xloc.bit_length() - 1
-    inline = lax.shift_right_logical(bins, xl_bits)
-    cross = bins & (xloc * nx - 1)
-    target = inline // il if il > 1 else inline
-    target = target * nx + lax.shift_right_logical(cross, loc_bits)
-    local_bin = cross & (xloc - 1)
-    if il > 1:
-        local_bin = local_bin + (inline % il) * xloc
-    pad_cols = jnp.zeros((shots, LANES - trs), F32)
-    table = jnp.concatenate(
-        [
-            jnp.concatenate([x.astype(F32), pad_cols], axis=1)
-            for x in (target + 1, local_bin + 1, slot_ref[...] + 1)
-        ]
-        + [jnp.zeros((8 - 3 * shots, LANES), F32)],
-        axis=0,
-    )
-    r_i, n_i = iota((LANES, LANES), 0), iota((LANES, LANES), 1)
-    order = jnp.where(r_i == GROUP * (n_i & (groups - 1)) + lax.shift_right_logical(n_i, 5), 1.0, 0.0)
-    table = exact(table, order.astype(F32))
-
-    def row(kind):
-        return jnp.concatenate([table[kind * shots + s : kind * shots + s + 1] for s in range(shots)], axis=1)
-
-    t_row = row(0).astype(jnp.int32) - 1
-    b_row, s_row = row(1), row(2)
-    onehot = (iota((nd, cols), 0) == t_row).astype(F32)
-    onehot_b = onehot.astype(BF16)
-    before = (iota((cols, cols), 0) < iota((cols, cols), 1)).astype(F32).astype(BF16)
-    rank = jnp.sum(onehot * dot(onehot_b, before), axis=0, keepdims=True)
-    rank = (rank + 0.5).astype(jnp.int32)
-    pick[...] = (iota((slots, cols), 0) == t_row * cap + rank).astype(F32).astype(BF16)
-    k_i = iota((LANES, cols), 0)
-    coded = jnp.where(
-        k_i == rank, b_row, jnp.where(k_i == rank + cap, s_row, jnp.zeros((LANES, cols), F32))
-    )
-    coded = jnp.where(k_i < 2 * cap, coded, 0.0)
-    outgoing_codes = rows_by_columns(onehot_b, coded.astype(BF16))
-    for d in range(nd):
-        code_send[d] = outgoing_codes[d : d + 1]
+    for copy in smalls:
+        copy.wait()
 
     for s in range(shots):
         base = jnp.concatenate([jnp.zeros((1, taps), F32), filt_ref[s : s + 1]], axis=1)
@@ -195,6 +178,34 @@
                 place = (s, pl.ds(kb * LANES, LANES), pl.ds(ib * LANES, LANES))
                 amat_h[place] = high
                 amat_l[place] = low
+
+    load.wait()
+    pl.semaphore_wait(barrier, len(y_peers) + len(z_peers) + len(x_peers))
+
+    def halo(side):
+        at = PAD if side == 0 else trs
+        to = PAD + trs if side == 0 else 0
+        return pltpu.make_async_remote_copy(
+            src_ref=xe.at[:, pl.ds(at, PAD), pl.ds(taps, samples)],
+            dst_ref=xe.at[:, pl.ds(to, PAD), pl.ds(taps, samples)],
+            send_sem=halo_ssem.at[side],
+            recv_sem=halo_rsem.at[side],
+            device_id=(bi, xi - 1 if side == 0 else xi + 1),
+            device_id_type=MESH,
+        )
+
+    has_left, has_right = xi > 0, xi < nx - 1
+
+    @pl.when(has_left)
+    def _():
+        halo(0).start()
+
+    @pl.when(has_right)
+    def _():
+        halo(1).start()
+
+    for peer in z_peers:
+        pl.semaphore_signal(stage_sem.at[0], inc=1, device_id=peer, device_id_type=MESH)
 
     dipx[...] = jnp.zeros(dipx.shape, F32)
     dipx[0:xtaps, 0:ltaps] = dip_ref[...]
@@ -224,33 +235,87 @@
             tmat_h[u * LANES : (u + 1) * LANES, at : at + LANES] = high
             tmat_l[u * LANES : (u + 1) * LANES, at : at + LANES] = low
 
-    load.wait()
-    pl.semaphore_wait(barrier, nd - 1)
-
-    def halo(side):
-        at = PAD if side == 0 else trs
-        to = PAD + trs if side == 0 else 0
-        return pltpu.make_async_remote_copy(
-            src_ref=xe.at[:, pl.ds(at, PAD), pl.ds(taps, samples)],
-            dst_ref=xe.at[:, pl.ds(to, PAD), pl.ds(taps, samples)],
-            send_sem=halo_ssem.at[side],
-            recv_sem=halo_rsem.at[side],
-            device_id=(bi, xi - 1 if side == 0 else xi + 1),
-            device_id_type=MESH,
-        )
-
-    has_left, has_right = xi > 0, xi < nx - 1
+    lane = iota((1, LANES), 1)
+    bins = bin_ref[...]
+    xl_bits = (xloc * nx).bit_length() - 1
+    loc_bits = xloc.bit_length() - 1
+    inline = lax.shift_right_logical(bins, xl_bits)
+    cross = bins & (xloc * nx - 1)
+    target = inline // il if il > 1 else inline
+    target = target * nx + lax.shift_right_logical(cross, loc_bits)
+    local_bin = cross & (xloc - 1)
+    if il > 1:
+        local_bin = local_bin + (inline % il) * xloc
+    pad_cols = jnp.zeros((shots, LANES - trs), F32)
+    table = jnp.concatenate(
+        [
+            jnp.concatenate([x.astype(F32), pad_cols], axis=1)
+            for x in (target + 1, local_bin + 1, slot_ref[...] + 1)
+        ]
+        + [jnp.zeros((8 - 3 * shots, LANES), F32)],
+        axis=0,
+    )
+    r_i, n_i = iota((LANES, LANES), 0), iota((LANES, LANES), 1)
+    order = jnp.where(r_i == GROUP * (n_i & (groups - 1)) + lax.shift_right_logical(n_i, 5), 1.0, 0.0)
+    table = exact(table, order.astype(F32))
+
+    def row(kind):
+        return jnp.concatenate([table[kind * shots + s : kind * shots + s + 1] for s in range(shots)], axis=1)
+
+    t_row = row(0).astype(jnp.int32) - 1
+    b_row, s_row = row(1), row(2)
+    onehot = (iota((nd, cols), 0) == t_row).astype(F32)
+    onehot_b = onehot.astype(BF16)
+    before = (iota((cols, cols), 0) < iota((cols, cols), 1)).astype(F32).astype(BF16)
+    rank = jnp.sum(onehot * dot(onehot_b, before), axis=0, keepdims=True)
+    rank = (rank + 0.5).astype(jnp.int32)
+    pick[...] = (iota((slots, cols), 0) == jnp.where(t_row < 0, -1, rank * nd + t_row)).astype(F32).astype(BF16)
+    k_i = iota((LANES, cols), 0)
+    coded = jnp.where(
+        k_i == rank, b_row, jnp.where(k_i == rank + cap, s_row, jnp.zeros((LANES, cols), F32))
+    )
+    coded = jnp.where(k_i < 2 * cap, coded, 0.0)
+    outgoing_codes = rows_by_columns(onehot_b, coded.astype(BF16))
+    for d in range(nd):
+        code_send[d] = outgoing_codes[d : d + 1]
+
+    @pl.when(has_right)
+    def _():
+        halo(0).wait_recv()
 
     @pl.when(has_left)
     def _():
-        halo(0).start()
-
-    @pl.when(has_right)
-    def _():
-        halo(1).start()
+        halo(1).wait_recv()
+
+    pl.semaphore_wait(stage_sem.at[0], len(z_peers))
+    for peer in x_peers:
+        pl.semaphore_signal(stage_sem.at[1], inc=1, device_id=peer, device_id_type=MESH)
+
+    rows = xe.shape[1]
+    l_b = iota((rows, LANES), 1)
+    right_mask, left_mask = l_b < LEFT, l_b < LANES - LEFT
+
+    def deconvolve(n):
+        for s in range(shots):
+            high, low = halves(
+                xe[s, :, pl.ds(pl.multiple_of(n * taps, taps), 2 * taps)]
+            )
+            got = dot3(high, low, amat_h[s], amat_l[s])
+            one, two = got[:, 0:LANES], got[:, LANES:]
+            one_r, two_r = pltpu.roll(one, LEFT, 1), pltpu.roll(two, LEFT, 1)
+            one_l, two_l = (pltpu.roll(v, LANES - LEFT, 1) for v in (one, two))
+            dec_a[s, 2 * n] = jnp.where(right_mask, last[s, 0], one_r)
+            dec_a[s, 2 * n + 1] = jnp.where(right_mask, one_r, two_r)
+            dec_b[s, 2 * n] = jnp.where(left_mask, last[s, 1], one_l)
+            dec_b[s, 2 * n + 1] = jnp.where(left_mask, one_l, two_l)
+            last[s, 0] = two_r
+            last[s, 1] = two_l
+
+    last[...] = jnp.zeros(last.shape, F32)
+    deconvolve(0)
 
     def send_codes(k, carry):
-        d = lax.rem(me + k, nd)
+        d = (me + k) & (nd - 1)
         pltpu.make_async_remote_copy(
             src_ref=code_send.at[d],
             dst_ref=code_recv.at[me],
@@ -261,71 +326,25 @@
         ).start()
         return carry
 
-    lax.fori_loop(1, nd, send_codes, 0)
-
-    dec[:, 0] = jnp.zeros((shots,) + dec.shape[2:], F32)
-    dec[:, blocks + 1] = jnp.zeros((shots,) + dec.shape[2:], F32)
-
-    def deconvolve(at, rows):
-        for s in range(shots):
-            window = xe[s, pl.ds(at, rows), :]
-            high, low = halves(window)
-            for n in range(samples // taps):
-                part = slice(n * taps, n * taps + 2 * taps)
-                got = dot3(high[:, part], low[:, part], amat_h[s], amat_l[s])
-                for e in range(taps // LANES):
-                    dec[s, 1 + n * (taps // LANES) + e, pl.ds(at, rows), :] = got[
-                        :, e * LANES : (e + 1) * LANES
-                    ]
-
-    deconvolve(PAD, trs + 0)
-
-    @pl.when(has_right)
-    def _():
-        halo(0).wait_recv()
-
-    @pl.when(has_left)
-    def _():
-        halo(1).wait_recv()
-
-    deconvolve(0, PAD)
-    deconvolve(PAD + trs, 2 * PAD)
-
-    @pl.when(has_left)
-    def _():
-        halo(0).wait_send()
-
-    @pl.when(has_right)
-    def _():
-        halo(1).wait_send()
-
-    def shift_block(e, carry):
-        for s in range(shots):
-            here = dec[s, e + 1]
-            l_b = iota(here.shape, 1)
-            dec_a[s, e] = jnp.where(
-                l_b < LEFT, pltpu.roll(dec[s, e], LEFT, 1), pltpu.roll(here, LEFT, 1)
-            )
-            dec_b[s, e] = jnp.where(
-                l_b < LANES - LEFT,
-                pltpu.roll(here, LANES - LEFT, 1),
-                pltpu.roll(dec[s, e + 2], LANES - LEFT, 1),
-            )
-        return carry
-
-    lax.fori_loop(0, blocks, shift_block, 0)
-
     per = CHUNK // LANES
-    sub = iota((8, LANES), 0)
 
     def dip_and_send(c, carry):
+        @pl.when(c < chunks - 1)
+        def _():
+            deconvolve(c + 1)
+
+        @pl.when(c == chunks - 1)
+        def _():
+            for s in range(shots):
+                dec_b[s, blocks] = jnp.where(left_mask, last[s, 1], 0.0)
+
         for s in range(shots):
             for e in range(per):
                 for parity, source in enumerate((dec_a, dec_b)):
                     at = ((s * per + e) * 2 + parity) * groups
                     for u in range(members):
                         piece = source[
-                            s, c * per + e, pl.ds(PAD - half + u, groups, stride=GROUP), :
+                            s, c * per + e + parity, pl.ds(PAD - half + u, groups, stride=GROUP), :
                         ]
                         high, low = halves(piece)
                         xh[at : at + groups, u * LANES : (u + 1) * LANES] = high
@@ -348,16 +367,21 @@
             columns.append(jnp.concatenate(stack, axis=0))
         high, low = halves(jnp.concatenate(columns, axis=1))
         packed = dot(pick[...], high) + dot(pick[...], low)
-        for pair in range(nd // 2):
-            a = packed[8 * pair : 8 * pair + 8, 0:LANES]
-            b = packed[8 * pair : 8 * pair + 8, LANES:]
-            send[c, 16 * pair : 16 * pair + 8] = jnp.where(sub < 4, a, pltpu.roll(b, 4, 0))
-            send[c, 16 * pair + 8 : 16 * pair + 16] = jnp.where(sub < 4, pltpu.roll(a, 4, 0), b)
+        for e in range(per):
+            for k in range(cap):
+                send[c, pl.ds(e * cap + k, nd, stride=8), :] = packed[
+                    k * nd : (k + 1) * nd, e * LANES : (e + 1) * LANES
+                ]
+
+        @pl.when(c == 0)
+        def _():
+            pl.semaphore_wait(stage_sem.at[1], len(x_peers))
+
         own = pl.ds(pl.multiple_of(me * 8, 8), 8)
         recv[c, own, :] = send[c, own, :]
 
         def start(k, carry):
-            d = lax.rem(me + k, nd)
+            d = (me + k) & (nd - 1)
             pltpu.make_async_remote_copy(
                 src_ref=send.at[c, pl.ds(pl.multiple_of(d * 8, 8), 8)],
                 dst_ref=recv.at[c, own],
@@ -369,6 +393,11 @@
             return carry
 
         lax.fori_loop(1, nd, start, 0)
+
+        @pl.when(c == 0)
+        def _():
+            lax.fori_loop(1, nd, send_codes, 0)
+
         return carry
 
     lax.fori_loop(0, chunks, dip_and_send, 0)
@@ -381,14 +410,9 @@
     for d in range(nd):
         codes[d : d + 1, :] = code_recv[d]
     eye = (iota((8, LANES), 0) == iota((8, LANES), 1)).astype(F32).astype(BF16)
-    by_slot = rows_by_columns(eye, codes[...].astype(BF16)).astype(BF16)
-    r_l = iota((nd, slots), 1)
-    spread = (lax.shift_right_logical(r_l, 2) == iota((nd, slots), 0)).astype(F32).astype(BF16)
-    spread = dot(by_slot, spread)
-    k_s = iota((8, slots), 0)
-    own_k = iota((8, slots), 1) & (cap - 1)
-    in_bin = jnp.sum(jnp.where(k_s == own_k, spread, 0.0), axis=0, keepdims=True) - 1.0
-    in_slot = jnp.sum(jnp.where(k_s == own_k + cap, spread, 0.0), axis=0, keepdims=True) - 1.0
+    by_slot = rows_by_columns(eye, codes[...].astype(BF16))
+    in_bin = jnp.concatenate([by_slot[k : k + 1] for k in range(cap)], axis=1) - 1.0
+    in_slot = jnp.concatenate([by_slot[k : k + 1] for k in range(cap, 2 * cap)], axis=1) - 1.0
     in_bin = jnp.where(in_bin < 0.0, in_bin - 0.5, in_bin + 0.5).astype(jnp.int32)
     in_slot = (in_slot + 1.5).astype(jnp.int32) - 1
     in_slot = jnp.where(in_bin < 0, -1000, in_slot)
@@ -438,14 +462,14 @@
     def gather(c, carry):
         some = recv.at[c, pl.ds(0, 8 * (nd - 1))]
         pltpu.make_async_copy(some, some, rsem.at[c]).wait()
-        first, second = [], []
-        for pair in range(nd // 2):
-            a = recv[c, 16 * pair : 16 * pair + 8]
-            b = recv[c, 16 * pair + 8 : 16 * pair + 16]
-            first.append(jnp.where(sub < 4, a, pltpu.roll(b, 4, 0)))
-            second.append(jnp.where(sub < 4, pltpu.roll(a, 4, 0), b))
         whole = jnp.concatenate(
-            [jnp.concatenate(first, axis=0), jnp.concatenate(second, axis=0)], axis=1
+            [
+                jnp.concatenate(
+                    [recv[c, pl.ds(e * cap + k, nd, stride=8), :] for k in range(cap)], axis=0
+                )
+                for e in range(per)
+            ],
+            axis=1,
         )
         high, low = halves(whole)
         edge = dot3(w_h[0 : 2 * LANES], w_l[0 : 2 * LANES], high, low)
@@ -463,11 +487,14 @@
         for b in range(xloc):
             at = (2 + b) * LANES
             outbuf[c, b] = dot3(w_h[at : at + LANES], w_l[at : at + LANES], high, low)[0:fold_cap]
+
+        @pl.when(c > 0)
+        def _():
+            finish(c - 1)
+
         return carry
 
-    lax.fori_loop(0, chunks, gather, 0)
-
-    def finish(c, carry):
+    def finish(c):
         @pl.when(has_right)
         def _():
             rim(c, 0).wait_recv()
@@ -479,7 +506,6 @@
             outbuf[c, 0] += rim_recv[c, 1]
 
         store(c).start()
-        return carry
 
     def store(c):
         return pltpu.make_async_copy(
@@ -488,7 +514,16 @@
             out_sem.at[c],
         )
 
-    lax.fori_loop(0, chunks, finish, 0)
+    lax.fori_loop(0, chunks, gather, 0)
+    finish(chunks - 1)
+
+    @pl.when(has_left)
+    def _():
+        halo(0).wait_send()
+
+    @pl.when(has_right)
+    def _():
+        halo(1).wait_send()
 
     def drain(c, carry):
         some = send.at[c, pl.ds(0, 8 * (nd - 1))]
@@ -522,25 +557,29 @@
     rows = trs + 3 * PAD
     slots = nd * cap
     m_rows = shots * (CHUNK // STEP) * 32
-    vmem = pl.BlockSpec(memory_space=pltpu.VMEM)
-    smem = pl.BlockSpec(memory_space=pltpu.SMEM)
-    hbm = pl.BlockSpec(memory_space=pl.ANY)
-    dma, regular = pltpu.SemaphoreType.DMA, pltpu.SemaphoreType.REGULAR
+    hbm = pl.BlockSpec(memory_space=pltpu.HBM)
+    dma = pltpu.SemaphoreType.DMA
     return pl.pallas_call(
         functools.partial(kernel, dims),
         out_shape=jax.ShapeDtypeStruct((il, xloc, fold_cap, samples), F32),
-        in_specs=[hbm, vmem, vmem, vmem, vmem, smem, smem],
+        in_specs=[hbm] * 7,
         out_specs=hbm,
         scratch_shapes=[
+            pltpu.VMEM(decon_filter.shape, F32),
+            pltpu.VMEM(dip_kernel.shape, F32),
+            pltpu.VMEM(bin_map.shape, jnp.int32),
+            pltpu.VMEM(slot.shape, jnp.int32),
+            pltpu.SMEM(cmp_kernel.shape, F32),
+            pltpu.SMEM(fold.shape, jnp.int32),
             pltpu.VMEM((shots, rows, taps + samples), F32),
             pltpu.VMEM((shots, 2 * taps, taps), BF16),
             pltpu.VMEM((shots, 2 * taps, taps), BF16),
             pltpu.VMEM((dip_kernel.shape[0] + 1, 2 * LANES), F32),
             pltpu.VMEM((members * LANES, 2 * LANES), BF16),
             pltpu.VMEM((members * LANES, 2 * LANES), BF16),
-            pltpu.VMEM((shots, blocks + 2, rows, LANES), F32),
+            pltpu.VMEM((shots, 2, rows, LANES), F32),
             pltpu.VMEM((shots, blocks, rows, LANES), F32),
-            pltpu.VMEM((shots, blocks, rows, LANES), F32),
+            pltpu.VMEM((shots, blocks + 1, rows, LANES), F32),
             pltpu.VMEM((m_rows, members * LANES), BF16),
             pltpu.VMEM((m_rows, members * LANES), BF16),
             pltpu.VMEM((slots, shots * LANES), BF16),
@@ -554,7 +593,9 @@
             pltpu.VMEM((chunks, 2, fold_cap, CHUNK), F32),
             pltpu.VMEM((chunks, 2, fold_cap, CHUNK), F32),
             pltpu.VMEM((chunks, xloc, fold_cap, CHUNK), F32),
+            pltpu.SemaphoreType.REGULAR((2,)),
             dma,
+            dma((6,)),
             dma((2,)),
             dma((2,)),
             dma,
@@ -566,7 +607,7 @@
             dma((chunks,)),
         ],
         compiler_params=pltpu.CompilerParams(
-            collective_id=0, has_side_effects=True, vmem_limit_bytes=48 << 20
+            collective_id=0, has_side_effects=True, vmem_limit_bytes=62 << 20
         ),
     )(traces, decon_filter, dip_kernel, bin_map, slot, cmp_kernel, fold)
 

time: 58.6 us -> 50.8 us (0.87)
  the two profiles are of different devices: /device:TPU:3 before, /device:TPU:1 now
where the time goes in v2:
time: 50.8 us; the launch traced here: 50.7 us
  Pallas kernels  47.6 us (94%)
  local copies, waits for them, and re-layouts  3.04 us (6%)
    pallas_call x1, Pallas kernels, local(): pl.pallas_call(functools.partial(kernel, dims), out_shape=jax.ShapeDtypeS...  47.6 us
    unnamed x1, local copies, waits for them, and re-layouts  3.04 us

profile of v2, /device:TPU:1, one launch (start us, length us, event | category | flops | bytes accessed | tf_op | source)
XLA Modules:
  0.0 50.7 jit_solution(4966045815553898737)
XLA Ops:
  0.0 47.6 %shard_map.73 = f32[1,4,120,1024]{3,2,1,0:T(8,128)} custom-call(f32[2,120,1024]{2,1,0:T(8,128)} %traces_ref.1, f32[2,256]{1,0:T(2,128)} %filt_hbm.1, f32[15,31]{1,0:T(8,128)} %dip_hbm.1, s32[2,120]{1,0:T(2,128)} %bin_hbm.1, s32[2,120]{1,0:T(2,128)} %slot_hbm.1, f32[3,5]{1,0:T(4,128)} %cmp_hbm.1, s32[1,4]{1,0:T(1,128)} %fold_hbm.1), custom_call_target="tpu_custom_call" | custom-call | tf_op jit(solution)/shard_map/pallas_call | solution.py:562
  47.6 3.0 %copy.9 = f32[1,4,120,1024]{3,2,1,0:T(8,128)} copy(f32[1,4,120,1024]{3,2,1,0:T(8,128)} %shard_map.73) | data formatting | bytes 3932160

commit v3 on v2

--- a/solution.py
+++ b/solution.py
@@ -42,6 +42,143 @@
 
 def rows_by_columns(a, b):
     return lax.dot_general(a, b, (((1,), (1,)), ((), ())), preferred_element_type=F32)
+
+
+def extended_2(array, sides, width):
+    for axis, dim in sides:
+        size, length = (lax.axis_size(axis), array.shape[dim])
+        up = [(i, (i + 1) % size) for i in range(size - 1)]
+        down = [(j, i) for i, j in up]
+        last = lax.slice_in_dim(array, length - width, length, axis=dim)
+        first = lax.slice_in_dim(array, 0, width, axis=dim)
+        before = lax.ppermute(last, axis, up)
+        after = lax.ppermute(first, axis, down)
+        array = jnp.concatenate([before, array, after], axis=dim)
+    return array
+
+
+def toeplitz(filt):
+    taps = filt.shape[-1]
+    lag_index = (
+        jnp.arange(128, dtype=jnp.int32)[None, :] + 256 - jnp.arange(384, dtype=jnp.int32)[:, None]
+    )
+    valid = (lag_index >= 0) & (lag_index < taps)
+    clipped = jnp.clip(lag_index, 0, taps - 1)
+    return jnp.where(valid, jnp.take(filt, clipped, axis=-1), jnp.float32(0.0))
+
+
+def sample_windows(data, front, back):
+    samples = data.shape[-1]
+    blocks_count = samples // 128
+    padding = [(0, 0)] * (data.ndim - 1) + [(front, back)]
+    padded = jnp.pad(data, padding)
+    blocks = padded.reshape(data.shape[:-1] + (blocks_count + 2, 128))
+    return jnp.concatenate(
+        [
+            blocks[..., 0:blocks_count, :],
+            blocks[..., 1 : blocks_count + 1, :],
+            blocks[..., 2 : blocks_count + 2, :],
+        ],
+        axis=-1,
+    )
+
+
+def deconvolve(data, matrices):
+    windows = sample_windows(data, 256, 0)
+    result = jnp.einsum("snbw,swi->snbi", windows, matrices, precision=lax.Precision.HIGHEST)
+    return result.reshape(data.shape)
+
+
+def rank_within(target, valid, dev_count):
+    onehot = (
+        (target[:, None] == jnp.arange(dev_count, dtype=jnp.int32)[None, :]) & valid[:, None]
+    ).astype(jnp.int32)
+    return jnp.sum(jnp.cumsum(onehot, axis=0) * onehot, axis=1) - 1
+
+
+def general(traces, decon_filter, dip_kernel, cmp_kernel, bin_map, slot, fold):
+    shot_count, tr_dev, samples = traces.shape
+    half = (dip_kernel.shape[0] - 1) // 2
+    lag_count = dip_kernel.shape[1]
+    lag_half = (lag_count - 1) // 2
+    matrices = toeplitz(decon_filter)
+    extended = extended_2(deconvolve(traces, matrices), (("xline", 1),), half)
+    sample_padded = jnp.pad(extended, ((0, 0), (0, 0), (lag_half, lag_half)))
+
+    def add_term(trace_tap, running):
+        sliced = lax.dynamic_slice_in_dim(sample_padded, trace_tap, tr_dev, 1)
+        weights = lax.dynamic_index_in_dim(dip_kernel, trace_tap, 0, keepdims=False)
+        for lag in range(lag_count):
+            running = running + weights[lag] * sliced[:, :, lag : lag + samples]
+        return running
+
+    start = jnp.zeros((shot_count, tr_dev, samples), jnp.float32)
+    filtered = lax.fori_loop(0, dip_kernel.shape[0], add_term, start).reshape(
+        shot_count * tr_dev, samples
+    )
+    bin_devices = lax.axis_size("bin")
+    cross_devices = lax.axis_size("xline")
+    dev_count = bin_devices * cross_devices
+    il_local, xl_local = fold.shape
+    per_device = shot_count * tr_dev
+    bins_local = il_local * xl_local
+    send_cap = 2 * ((per_device + dev_count - 1) // dev_count)
+    fold_cap = 2 * ((per_device + bins_local - 1) // bins_local)
+    cross_total = xl_local * cross_devices
+    global_bin = bin_map.reshape(per_device)
+    slot_flat = slot.reshape(per_device)
+    inline = global_bin // cross_total
+    cross_bin = global_bin % cross_total
+    bin_dev = inline // il_local
+    cross_dev = cross_bin // xl_local
+    il_in = inline % il_local
+    xl_in = cross_bin % xl_local
+    target = bin_dev * cross_devices + cross_dev
+    always = jnp.ones((per_device,), jnp.bool_)
+    dest_rank = rank_within(target, always, dev_count)
+    cross_half = (cmp_kernel.shape[0] - 1) // 2
+    offset_half = (cmp_kernel.shape[1] - 1) // 2
+    buffer_rows = bins_local * fold_cap
+    slot_code = (il_in * xl_local + xl_in) * fold_cap + slot_flat
+    send_row = target * send_cap + dest_rank
+    outgoing = jnp.zeros((dev_count * send_cap, samples), jnp.float32).at[send_row].set(filtered)
+    out_codes = (
+        jnp.full((dev_count * send_cap,), buffer_rows, jnp.int32).at[send_row].set(slot_code)
+    )
+    received, recv_codes = (
+        lax.all_to_all(
+            outgoing.reshape(dev_count, send_cap, samples),
+            ("bin", "xline"),
+            split_axis=0,
+            concat_axis=0,
+            tiled=True,
+        ),
+        lax.all_to_all(
+            out_codes.reshape(dev_count, send_cap),
+            ("bin", "xline"),
+            split_axis=0,
+            concat_axis=0,
+            tiled=True,
+        ),
+    )
+    gathers = (
+        jnp.zeros((buffer_rows, samples), jnp.float32)
+        .at[recv_codes.reshape(-1)]
+        .set(received.reshape(-1, samples), mode="drop")
+    )
+    fold_scale = lax.rsqrt(jnp.maximum(fold, 1).astype(jnp.float32))
+    normed = gathers.reshape(il_local, xl_local, fold_cap, samples) * fold_scale[:, :, None, None]
+    with_rims = extended_2(normed, (("xline", 1),), cross_half)
+    padded = jnp.pad(with_rims, ((0, 0), (0, 0), (offset_half, offset_half), (0, 0)))
+    result = jnp.zeros((il_local, xl_local, fold_cap, samples), jnp.float32)
+    for cross_tap in range(cmp_kernel.shape[0]):
+        for offset_tap in range(cmp_kernel.shape[1]):
+            result = (
+                result
+                + cmp_kernel[cross_tap, offset_tap]
+                * padded[:, cross_tap : cross_tap + xl_local, offset_tap : offset_tap + fold_cap, :]
+            )
+    return result
 
 
 def kernel(
@@ -54,6 +191,7 @@
     cmp_hbm,
     fold_hbm,
     out_ref,
+    flag_ref,
     filt_ref,
     dip_ref,
     bin_ref,
@@ -75,6 +213,13 @@
     code_send,
     code_recv,
     codes,
+    far_send,
+    far_recv,
+    far_rows,
+    near_send,
+    near_recv,
+    near_rows,
+    taken,
     send,
     recv,
     w_h,
@@ -89,6 +234,10 @@
     halo_rsem,
     code_ssem,
     code_rsem,
+    far_ssem,
+    far_rsem,
+    near_ssem,
+    near_rsem,
     ssem,
     rsem,
     rim_ssem,
@@ -99,6 +248,9 @@
     nd = nb * nx
     blocks = samples // LANES
     chunks = samples // CHUNK
+    direct = cap - 1
+    per = CHUNK // LANES
+    held = direct * per
     bi, xi = lax.axis_index("bin"), lax.axis_index("xline")
     me = bi * nx + xi
     taps = filt_ref.shape[1]
@@ -107,7 +259,7 @@
     half = (xtaps - 1) // 2
     members = xtaps + GROUP - 1
     groups = 32
-    slots = nd * cap
+    slots = nd * direct + LANES
     cols = shots * LANES
 
     def device(d):
@@ -269,13 +421,28 @@
     before = (iota((cols, cols), 0) < iota((cols, cols), 1)).astype(F32).astype(BF16)
     rank = jnp.sum(onehot * dot(onehot_b, before), axis=0, keepdims=True)
     rank = (rank + 0.5).astype(jnp.int32)
-    pick[...] = (iota((slots, cols), 0) == jnp.where(t_row < 0, -1, rank * nd + t_row)).astype(F32).astype(BF16)
+    extra = (t_row >= 0) & (rank >= direct)
+    straight = (t_row >= 0) & (rank < direct)
+    place = jnp.where(extra, nd * direct, jnp.where(straight, rank * nd + t_row, -1))
+    pick[...] = (iota(pick.shape, 0) == place).astype(F32).astype(BF16)
+    extras = jnp.where(extra, 1.0, 0.0)
+    count = jnp.sum(extras, axis=1, keepdims=True)
+    extra_dest = jnp.sum(extras * (t_row + 1).astype(F32), axis=1, keepdims=True)
+    extra_bin = jnp.sum(extras * b_row, axis=1, keepdims=True)
+    extra_slot = jnp.sum(extras * s_row, axis=1, keepdims=True)
+    info = jnp.where(lane == 1, extra_bin, jnp.where(lane == 2, extra_slot, 0.0))
+    info = jnp.where(lane == 0, extra_dest, info)
+    for c in range(chunks):
+        far_send[c, 0] = info
     k_i = iota((LANES, cols), 0)
     coded = jnp.where(
         k_i == rank, b_row, jnp.where(k_i == rank + cap, s_row, jnp.zeros((LANES, cols), F32))
     )
     coded = jnp.where(k_i < 2 * cap, coded, 0.0)
     outgoing_codes = rows_by_columns(onehot_b, coded.astype(BF16))
+    outgoing_codes = jnp.where(
+        lane == 2 * cap, count, jnp.where(lane == 2 * cap + 1, extra_dest, outgoing_codes)
+    )
     for d in range(nd):
         code_send[d] = outgoing_codes[d : d + 1]
 
@@ -326,7 +493,69 @@
         ).start()
         return carry
 
-    per = CHUNK // LANES
+    far_rows[...] = jnp.zeros(far_rows.shape, F32)
+    near_rows[...] = jnp.zeros(near_rows.shape, F32)
+
+    def start_far(c):
+        far_recv[c, bi] = far_send[c]
+
+        def start(k, carry):
+            pltpu.make_async_remote_copy(
+                src_ref=far_send.at[c],
+                dst_ref=far_recv.at[c, bi],
+                send_sem=far_ssem.at[c],
+                recv_sem=far_rsem.at[c],
+                device_id=((bi + k) & (nb - 1), xi),
+                device_id_type=MESH,
+            ).start()
+            return carry
+
+        lax.fori_loop(1, nb, start, 0)
+
+    def wait_far(c, sem):
+        some = far_recv.at[c, pl.ds(0, nb - 1)]
+        pltpu.make_async_copy(some, some, sem.at[c]).wait()
+
+    def start_near(c):
+        wait_far(c, far_rsem)
+        for r in range(per + 1):
+            for b in range(nb):
+                far_rows[b : b + 1, r * LANES : (r + 1) * LANES] = far_recv[c, b, r]
+        eye = (iota((16, LANES), 0) == iota((16, LANES), 1)).astype(F32).astype(BF16)
+        dest = rows_by_columns(eye, far_rows[:, 0:LANES].astype(BF16))[0:1]
+        x_i = iota((16, LANES), 0)
+        select = (dest == (bi * nx + x_i + 1).astype(F32)) & (x_i < nx)
+        select = select.astype(F32).astype(BF16)
+        high, low = halves(far_rows[...])
+        got = dot(select, high) + dot(select, low)
+        for x in range(nx):
+            for r in range(per + 1):
+                near_send[c, x, r] = got[x : x + 1, r * LANES : (r + 1) * LANES]
+        near_recv[c, xi] = near_send[c, xi]
+
+        def start(k, carry):
+            x = (xi + k) & (nx - 1)
+            pltpu.make_async_remote_copy(
+                src_ref=near_send.at[c, x],
+                dst_ref=near_recv.at[c, xi],
+                send_sem=near_ssem.at[c],
+                recv_sem=near_rsem.at[c],
+                device_id=(bi, x),
+                device_id_type=MESH,
+            ).start()
+            return carry
+
+        lax.fori_loop(1, nx, start, 0)
+
+    def wait_near(c, sem):
+        some = near_recv.at[c, pl.ds(0, nx - 1)]
+        pltpu.make_async_copy(some, some, sem.at[c]).wait()
+
+    def take_near(c):
+        wait_near(c, near_rsem)
+        for r in range(per + 1):
+            for x in range(nx):
+                near_rows[x : x + 1, r * LANES : (r + 1) * LANES] = near_recv[c, x, r]
 
     def dip_and_send(c, carry):
         @pl.when(c < chunks - 1)
@@ -366,25 +595,27 @@
                         stack.append(jnp.where(l_g < STEP, pltpu.roll(even, STEP, 1), odd))
             columns.append(jnp.concatenate(stack, axis=0))
         high, low = halves(jnp.concatenate(columns, axis=1))
+        pair = [slice(e * LANES, (e + 1) * LANES) for e in range(per)]
         packed = dot(pick[...], high) + dot(pick[...], low)
         for e in range(per):
-            for k in range(cap):
-                send[c, pl.ds(e * cap + k, nd, stride=8), :] = packed[
-                    k * nd : (k + 1) * nd, e * LANES : (e + 1) * LANES
-                ]
+            for k in range(direct):
+                taken[pl.ds(e * direct + k, nd, stride=8), :] = packed[k * nd : (k + 1) * nd, pair[e]]
+            far_send[c, e + 1] = packed[nd * direct : nd * direct + 1, pair[e]]
+        for d in range(nd):
+            send[c, d] = taken[8 * d : 8 * d + held, :]
 
         @pl.when(c == 0)
         def _():
             pl.semaphore_wait(stage_sem.at[1], len(x_peers))
 
-        own = pl.ds(pl.multiple_of(me * 8, 8), 8)
-        recv[c, own, :] = send[c, own, :]
+        recv[c, me] = send[c, me]
+        start_far(c)
 
         def start(k, carry):
             d = (me + k) & (nd - 1)
             pltpu.make_async_remote_copy(
-                src_ref=send.at[c, pl.ds(pl.multiple_of(d * 8, 8), 8)],
-                dst_ref=recv.at[c, own],
+                src_ref=send.at[c, d],
+                dst_ref=recv.at[c, me],
                 send_sem=ssem.at[c],
                 recv_sem=rsem.at[c],
                 device_id=device(d),
@@ -397,6 +628,10 @@
         @pl.when(c == 0)
         def _():
             lax.fori_loop(1, nd, send_codes, 0)
+
+        @pl.when(c > 0)
+        def _():
+            start_near(c - 1)
 
         return carry
 
@@ -409,10 +644,20 @@
     pltpu.make_async_copy(some, some, code_ssem).wait()
     for d in range(nd):
         codes[d : d + 1, :] = code_recv[d]
-    eye = (iota((8, LANES), 0) == iota((8, LANES), 1)).astype(F32).astype(BF16)
+    eye = (iota((16, LANES), 0) == iota((16, LANES), 1)).astype(F32).astype(BF16)
     by_slot = rows_by_columns(eye, codes[...].astype(BF16))
-    in_bin = jnp.concatenate([by_slot[k : k + 1] for k in range(cap)], axis=1) - 1.0
-    in_slot = jnp.concatenate([by_slot[k : k + 1] for k in range(cap, 2 * cap)], axis=1) - 1.0
+    theirs, mine = by_slot[2 * cap + 1 : 2 * cap + 2], codes[:, 2 * cap + 1 : 2 * cap + 2]
+    s_i, s_j = iota((nd, nd), 0), iota((nd, nd), 1)
+    meet = (theirs == mine) & (mine > 0.5) & (s_i != s_j) & ((s_i & (nx - 1)) == (s_j & (nx - 1)))
+    bad = jnp.where(meet | (codes[:, 2 * cap : 2 * cap + 1] > 1.5), 1.0, 0.0)
+    flag_ref[0, 0] = jnp.max(bad).astype(jnp.int32)
+
+    take_near(0)
+    by_hop = rows_by_columns(eye, near_rows[:, 0:LANES].astype(BF16))
+    in_bin = [by_slot[k : k + 1] for k in range(direct)] + [by_hop[1:2]]
+    in_bin = jnp.concatenate(in_bin, axis=1) - 1.0
+    in_slot = [by_slot[k : k + 1] for k in range(cap, cap + direct)] + [by_hop[2:3]]
+    in_slot = jnp.concatenate(in_slot, axis=1) - 1.0
     in_bin = jnp.where(in_bin < 0.0, in_bin - 0.5, in_bin + 0.5).astype(jnp.int32)
     in_slot = (in_slot + 1.5).astype(jnp.int32) - 1
     in_slot = jnp.where(in_bin < 0, -1000, in_slot)
@@ -460,12 +705,21 @@
         )
 
     def gather(c, carry):
-        some = recv.at[c, pl.ds(0, 8 * (nd - 1))]
+        some = recv.at[c, pl.ds(0, nd - 1)]
         pltpu.make_async_copy(some, some, rsem.at[c]).wait()
+
+        @pl.when(c > 0)
+        def _():
+            take_near(c)
+
+        for d in range(nd):
+            taken[8 * d : 8 * d + held, :] = recv[c, d]
         whole = jnp.concatenate(
             [
                 jnp.concatenate(
-                    [recv[c, pl.ds(e * cap + k, nd, stride=8), :] for k in range(cap)], axis=0
+                    [taken[pl.ds(e * direct + k, nd, stride=8), :] for k in range(direct)]
+                    + [near_rows[:, (e + 1) * LANES : (e + 2) * LANES]],
+                    axis=0,
                 )
                 for e in range(per)
             ],
@@ -488,6 +742,10 @@
             at = (2 + b) * LANES
             outbuf[c, b] = dot3(w_h[at : at + LANES], w_l[at : at + LANES], high, low)[0:fold_cap]
 
+        @pl.when(c == 0)
+        def _():
+            start_near(chunks - 1)
+
         @pl.when(c > 0)
         def _():
             finish(c - 1)
@@ -526,8 +784,10 @@
         halo(1).wait_send()
 
     def drain(c, carry):
-        some = send.at[c, pl.ds(0, 8 * (nd - 1))]
+        some = send.at[c, pl.ds(0, nd - 1)]
         pltpu.make_async_copy(some, some, ssem.at[c]).wait()
+        wait_far(c, far_ssem)
+        wait_near(c, near_ssem)
 
         @pl.when(has_left)
         def _():
@@ -555,15 +815,20 @@
     members = dip_kernel.shape[0] + GROUP - 1
     blocks, chunks = samples // LANES, samples // CHUNK
     rows = trs + 3 * PAD
-    slots = nd * cap
+    slots = nd * (cap - 1) + LANES
+    per = CHUNK // LANES
+    held = (cap - 1) * per
     m_rows = shots * (CHUNK // STEP) * 32
     hbm = pl.BlockSpec(memory_space=pltpu.HBM)
     dma = pltpu.SemaphoreType.DMA
-    return pl.pallas_call(
+    fast, flag = pl.pallas_call(
         functools.partial(kernel, dims),
-        out_shape=jax.ShapeDtypeStruct((il, xloc, fold_cap, samples), F32),
+        out_shape=(
+            jax.ShapeDtypeStruct((il, xloc, fold_cap, samples), F32),
+            jax.ShapeDtypeStruct((1, 1), jnp.int32),
+        ),
         in_specs=[hbm] * 7,
-        out_specs=hbm,
+        out_specs=(hbm, pl.BlockSpec(memory_space=pltpu.SMEM)),
         scratch_shapes=[
             pltpu.VMEM(decon_filter.shape, F32),
             pltpu.VMEM(dip_kernel.shape, F32),
@@ -582,12 +847,19 @@
             pltpu.VMEM((shots, blocks + 1, rows, LANES), F32),
             pltpu.VMEM((m_rows, members * LANES), BF16),
             pltpu.VMEM((m_rows, members * LANES), BF16),
-            pltpu.VMEM((slots, shots * LANES), BF16),
+            pltpu.VMEM((nd * (cap - 1) + 16, shots * LANES), BF16),
             pltpu.VMEM((nd, 1, LANES), F32),
             pltpu.VMEM((nd, 1, LANES), F32),
             pltpu.VMEM((nd, LANES), F32),
-            pltpu.VMEM((chunks, nd * 8, LANES), F32),
-            pltpu.VMEM((chunks, nd * 8, LANES), F32),
+            pltpu.VMEM((chunks, per + 1, 1, LANES), F32),
+            pltpu.VMEM((chunks, nb, per + 1, 1, LANES), F32),
+            pltpu.VMEM((LANES, (per + 1) * LANES), F32),
+            pltpu.VMEM((chunks, nx, per + 1, 1, LANES), F32),
+            pltpu.VMEM((chunks, nx, per + 1, 1, LANES), F32),
+            pltpu.VMEM((LANES, (per + 1) * LANES), F32),
+            pltpu.VMEM((nd * 8, LANES), F32),
+            pltpu.VMEM((chunks, nd, held, LANES), F32),
+            pltpu.VMEM((chunks, nd, held, LANES), F32),
             pltpu.VMEM(((xloc + 2) * LANES, slots), BF16),
             pltpu.VMEM(((xloc + 2) * LANES, slots), BF16),
             pltpu.VMEM((chunks, 2, fold_cap, CHUNK), F32),
@@ -602,6 +874,10 @@
             dma,
             dma((chunks,)),
             dma((chunks,)),
+            dma((chunks,)),
+            dma((chunks,)),
+            dma((chunks,)),
+            dma((chunks,)),
             dma((chunks, 2)),
             dma((chunks, 2)),
             dma((chunks,)),
@@ -610,6 +886,12 @@
             collective_id=0, has_side_effects=True, vmem_limit_bytes=62 << 20
         ),
     )(traces, decon_filter, dip_kernel, bin_map, slot, cmp_kernel, fold)
+    return lax.cond(
+        flag[0, 0] > 0,
+        general,
+        lambda *args: fast,
+        *(traces, decon_filter, dip_kernel, cmp_kernel, bin_map, slot, fold),
+    )
 
 
 def solution(mesh):

time: 50.8 us -> 46.5 us (0.915)
  Pallas kernels: 47.6 us -> 44.1 us
  local copies, waits for them, and re-layouts: 3.04 us -> 1.27 us
  between operations: 0.01 us -> 0.64 us
    pallas_call x1, Pallas kernels: 47.6 us -> 44.1 us  [local(): pl.pallas_call(functools.partial(kernel, dims), out_shape=(jax.ShapeDtype...]
    unnamed x1, local copies, waits for them, and re-layouts: 3.04 us -> 1.27 us
where the time goes in v3:
time: 46.5 us; the launch traced here: 46.2 us
  Pallas kernels  44.1 us (95%)
  local copies, waits for them, and re-layouts  1.27 us (3%)
  between operations  0.64 us (1%)
    pallas_call x1, Pallas kernels, local(): pl.pallas_call(functools.partial(kernel, dims), out_shape=(jax.ShapeDtype...  44.1 us
    unnamed x1, local copies, waits for them, and re-layouts  1.27 us

profile of v3, /device:TPU:1, one launch (start us, length us, event | category | flops | bytes accessed | tf_op | source)
XLA Modules:
  0.0 46.2 jit_solution(10468083826560390657)
XLA Ops:
  0.0 44.1 %shard_map.75 = (f32[1,4,120,1024]{3,2,1,0:T(8,128)S(1)}, s32[1,1]{1,0:T(1,128)}) custom-call(f32[2,120,1024]{2,1,0:T(8,128)} %traces_ref.1, f32[2,256]{1,0:T(2,128)} %filt_hbm.1, f32[15,31]{1,0:T(8,128)} %dip_hbm.1, s32[2,120]{1,0:T(2,128)} %bin_hbm.1, s32[2,120]{1,0:T(2,128)} %slot_hbm.1, f32[3,5]{1,0:T(4,128)} %cmp_hbm.1, s32[1,4]{1,0:T(1,128)} %fold_hbm.1), custom_call_target="tpu_custom_call" | custom-call | tf_op jit(solution)/shard_map/pallas_call | solution.py:824
  44.7 0.2 conditional.1
  44.9 1.3 %copy.44 = f32[1,4,120,1024]{3,2,1,0:T(8,128)} copy(f32[1,4,120,1024]{3,2,1,0:T(8,128)S(1)} %get-tuple-element.113) | data formatting | bytes 3932160

commit v4 on v3

--- a/solution.py
+++ b/solution.py
@@ -482,7 +482,7 @@
     deconvolve(0)
 
     def send_codes(k, carry):
-        d = (me + k) & (nd - 1)
+        d = (me + 37 * k) & (nd - 1)
         pltpu.make_async_remote_copy(
             src_ref=code_send.at[d],
             dst_ref=code_recv.at[me],
@@ -612,7 +612,7 @@
         start_far(c)
 
         def start(k, carry):
-            d = (me + k) & (nd - 1)
+            d = (me + 37 * k) & (nd - 1)
             pltpu.make_async_remote_copy(
                 src_ref=send.at[c, d],
                 dst_ref=recv.at[c, me],

time: 46.5 us -> 45.5 us (0.978)
  Pallas kernels: 44.1 us -> 43.2 us
    pallas_call x1, Pallas kernels: 44.1 us -> 43.2 us  [local(): pl.pallas_call(functools.partial(kernel, dims), out_shape=(jax.ShapeDtype...]
where the time goes in v4:
time: 45.5 us; the launch traced here: 45.4 us
  Pallas kernels  43.2 us (95%)
  local copies, waits for them, and re-layouts  1.27 us (3%)
  between operations  0.64 us (1%)
    pallas_call x1, Pallas kernels, local(): pl.pallas_call(functools.partial(kernel, dims), out_shape=(jax.ShapeDtype...  43.2 us
    unnamed x1, local copies, waits for them, and re-layouts  1.27 us

profile of v4, /device:TPU:1, one launch (start us, length us, event | category | flops | bytes accessed | tf_op | source)
XLA Modules:
  0.0 45.4 jit_solution(141380459963375100)
XLA Ops:
  0.0 43.2 %shard_map.75 = (f32[1,4,120,1024]{3,2,1,0:T(8,128)S(1)}, s32[1,1]{1,0:T(1,128)}) custom-call(f32[2,120,1024]{2,1,0:T(8,128)} %traces_ref.1, f32[2,256]{1,0:T(2,128)} %filt_hbm.1, f32[15,31]{1,0:T(8,128)} %dip_hbm.1, s32[2,120]{1,0:T(2,128)} %bin_hbm.1, s32[2,120]{1,0:T(2,128)} %slot_hbm.1, f32[3,5]{1,0:T(4,128)} %cmp_hbm.1, s32[1,4]{1,0:T(1,128)} %fold_hbm.1), custom_call_target="tpu_custom_call" | custom-call | tf_op jit(solution)/shard_map/pallas_call | solution.py:824
  43.9 0.2 conditional.1
  44.1 1.3 %copy.44 = f32[1,4,120,1024]{3,2,1,0:T(8,128)} copy(f32[1,4,120,1024]{3,2,1,0:T(8,128)S(1)} %get-tuple-element.113) | data formatting | bytes 3932160

commit v5 on v4

--- a/solution.py
+++ b/solution.py
@@ -462,6 +462,11 @@
     l_b = iota((rows, LANES), 1)
     right_mask, left_mask = l_b < LEFT, l_b < LANES - LEFT
 
+    def keep(ref, s, at, value):
+        high = value.astype(BF16).astype(F32)
+        ref[0, s, at] = high
+        ref[1, s, at] = value - high
+
     def deconvolve(n):
         for s in range(shots):
             high, low = halves(
@@ -471,10 +476,10 @@
             one, two = got[:, 0:LANES], got[:, LANES:]
             one_r, two_r = pltpu.roll(one, LEFT, 1), pltpu.roll(two, LEFT, 1)
             one_l, two_l = (pltpu.roll(v, LANES - LEFT, 1) for v in (one, two))
-            dec_a[s, 2 * n] = jnp.where(right_mask, last[s, 0], one_r)
-            dec_a[s, 2 * n + 1] = jnp.where(right_mask, one_r, two_r)
-            dec_b[s, 2 * n] = jnp.where(left_mask, last[s, 1], one_l)
-            dec_b[s, 2 * n + 1] = jnp.where(left_mask, one_l, two_l)
+            keep(dec_a, s, 2 * n, jnp.where(right_mask, last[s, 0], one_r))
+            keep(dec_a, s, 2 * n + 1, jnp.where(right_mask, one_r, two_r))
+            keep(dec_b, s, 2 * n, jnp.where(left_mask, last[s, 1], one_l))
+            keep(dec_b, s, 2 * n + 1, jnp.where(left_mask, one_l, two_l))
             last[s, 0] = two_r
             last[s, 1] = two_l
 
@@ -565,19 +570,18 @@
         @pl.when(c == chunks - 1)
         def _():
             for s in range(shots):
-                dec_b[s, blocks] = jnp.where(left_mask, last[s, 1], 0.0)
+                keep(dec_b, s, blocks, jnp.where(left_mask, last[s, 1], 0.0))
 
         for s in range(shots):
             for e in range(per):
                 for parity, source in enumerate((dec_a, dec_b)):
                     at = ((s * per + e) * 2 + parity) * groups
                     for u in range(members):
-                        piece = source[
-                            s, c * per + e + parity, pl.ds(PAD - half + u, groups, stride=GROUP), :
-                        ]
-                        high, low = halves(piece)
-                        xh[at : at + groups, u * LANES : (u + 1) * LANES] = high
-                        xl[at : at + groups, u * LANES : (u + 1) * LANES] = low
+                        rows_u = pl.ds(PAD - half + u, groups, stride=GROUP)
+                        high = source[0, s, c * per + e + parity, rows_u, :]
+                        low = source[1, s, c * per + e + parity, rows_u, :]
+                        xh[at : at + groups, u * LANES : (u + 1) * LANES] = high.astype(BF16)
+                        xl[at : at + groups, u * LANES : (u + 1) * LANES] = low.astype(BF16)
         got = dot3(xh[...], xl[...], tmat_h[...], tmat_l[...])
         columns = []
         l_g = iota((groups, LANES), 1)
@@ -625,7 +629,7 @@
 
         lax.fori_loop(1, nd, start, 0)
 
-        @pl.when(c == 0)
+        @pl.when(c == 1)
         def _():
             lax.fori_loop(1, nd, send_codes, 0)
 
@@ -843,8 +847,8 @@
             pltpu.VMEM((members * LANES, 2 * LANES), BF16),
             pltpu.VMEM((members * LANES, 2 * LANES), BF16),
             pltpu.VMEM((shots, 2, rows, LANES), F32),
-            pltpu.VMEM((shots, blocks, rows, LANES), F32),
-            pltpu.VMEM((shots, blocks + 1, rows, LANES), F32),
+            pltpu.VMEM((2, shots, blocks, rows, LANES), F32),
+            pltpu.VMEM((2, shots, blocks + 1, rows, LANES), F32),
             pltpu.VMEM((m_rows, members * LANES), BF16),
             pltpu.VMEM((m_rows, members * LANES), BF16),
             pltpu.VMEM((nd * (cap - 1) + 16, shots * LANES), BF16),

time: 45.5 us -> 45.5 us (level)
  no operation moved by 1% of the time
where the time goes in v5:
time: 45.5 us; the launch traced here: 45.3 us
  Pallas kernels  43.2 us (95%)
  local copies, waits for them, and re-layouts  1.27 us (3%)
  between operations  0.64 us (1%)
    pallas_call x1, Pallas kernels, local(): pl.pallas_call(functools.partial(kernel, dims), out_shape=(jax.ShapeDtype...  43.2 us
    unnamed x1, local copies, waits for them, and re-layouts  1.27 us

profile of v5, /device:TPU:1, one launch (start us, length us, event | category | flops | bytes accessed | tf_op | source)
XLA Modules:
  0.0 45.3 jit_solution(17995639960551687427)
XLA Ops:
  0.0 43.2 %shard_map.75 = (f32[1,4,120,1024]{3,2,1,0:T(8,128)S(1)}, s32[1,1]{1,0:T(1,128)}) custom-call(f32[2,120,1024]{2,1,0:T(8,128)} %traces_ref.1, f32[2,256]{1,0:T(2,128)} %filt_hbm.1, f32[15,31]{1,0:T(8,128)} %dip_hbm.1, s32[2,120]{1,0:T(2,128)} %bin_hbm.1, s32[2,120]{1,0:T(2,128)} %slot_hbm.1, f32[3,5]{1,0:T(4,128)} %cmp_hbm.1, s32[1,4]{1,0:T(1,128)} %fold_hbm.1), custom_call_target="tpu_custom_call" | custom-call | tf_op jit(solution)/shard_map/pallas_call | solution.py:828
  43.8 0.2 conditional.1
  44.1 1.3 %copy.44 = f32[1,4,120,1024]{3,2,1,0:T(8,128)} copy(f32[1,4,120,1024]{3,2,1,0:T(8,128)S(1)} %get-tuple-element.113) | data formatting | bytes 3932160
